TPU v7x, 32 devices: a whole 2x2x4 slice. The times are simulated.
32 devices in a mesh: lat: 2 (over x), lon: 4 (over z), ch: 4 (over y, core).
Axes of the slice: x: 2, y: 2, z: 4, core: 2. Of those that a mesh axis runs over, the one named last changes fastest.
Arguments:
- features: bfloat16 [1, 14, 96, 1024], P(None, 'lat', 'lon', 'ch'), may hold values from -6 to 6
- kernel_one: bfloat16 [3, 3, 4, 256, 1024], P(None, None, 'ch', 'lon'), may hold values from -0.0625 to 0.0625
- bias_one: float32 [1024], P('ch'), may hold values from -3 to 3
- kernel_two: bfloat16 [3, 3, 4, 256, 1024], P(None, None, 'ch', 'lon'), may hold values from -0.0625 to 0.0625
- bias_two: float32 [1024], P('ch'), may hold values from -3 to 3
Outputs:
- outputs: bfloat16 [1, 14, 96, 1024], P(None, 'lat', 'lon', 'ch')
All inputs are finite; a program needn't handle non-finite values.
Results may differ from a plain program's by a relative error of at most 0.01.
Values may be sent and summed in bfloat16 or wider, within the bound.
A program may use at most 64 MiB of HBM per device.

v0:
```python
import jax
import jax.numpy as jnp
from jax import lax
from jax.sharding import PartitionSpec as P

skip_scale = 0.7071067811865476


def extended(array, sides, width, wrap):
    for axis, dim in sides:
        peers, length = (lax.axis_size(axis), array.shape[dim])
        up = [(i, (i + 1) % peers) for i in range(peers if wrap else peers - 1)]
        down = [(j, i) for i, j in up]
        last = lax.slice_in_dim(array, length - width, length, axis=dim)
        leading = lax.slice_in_dim(array, 0, width, axis=dim)
        before = lax.ppermute(last, axis, up)
        after = lax.ppermute(leading, axis, down)
        array = jnp.concatenate([before, array, after], axis=dim)
    return array


def shifted(block, axis, distance):
    devices = range(lax.axis_size(axis))
    route = [((i - distance) % len(devices), i) for i in devices]
    return lax.ppermute(block, axis, route)


def apply_taps(padded, kernel):
    count_items = padded.shape[0]
    height = padded.shape[1] - 2
    breadth = padded.shape[2] - 2
    channels = padded.shape[3]
    accumulated = jnp.zeros((count_items * height * breadth, kernel.shape[3]), jnp.float32)
    for row_off in range(3):
        for col_off in range(3):
            window = padded[:, row_off : row_off + height, col_off : col_off + breadth].reshape(
                -1, channels
            )
            accumulated = accumulated + jnp.dot(
                window, kernel[row_off, col_off], preferred_element_type=jnp.float32
            )
    return accumulated.reshape(count_items, height, breadth, kernel.shape[3])


def fold_pad(source):
    north_south = extended(source, (("lat", 1),), 1, False)
    pole_pair = jnp.concatenate([source[:, :1], source[:, -1:]], axis=1)
    pole_pair = shifted(pole_pair, "lon", lax.axis_size("lon") // 2)
    band_idx = lax.axis_index("lat")
    first_row = jnp.where(band_idx == 0, pole_pair[:, :1], north_south[:, :1])
    last_row = jnp.where(
        band_idx == lax.axis_size("lat") - 1, pole_pair[:, 1:], north_south[:, -1:]
    )
    banded = jnp.concatenate([first_row, north_south[:, 1:-1], last_row], axis=1)
    return extended(banded, (("lon", 2),), 1, True)


def conv_sum(activation, kernel, bias_vec):
    padded = fold_pad(activation)
    out_width = kernel.shape[4]
    piece = lax.all_gather(kernel, "lon", axis=3, tiled=True)
    count_rows = piece.shape[3]
    partial_value = apply_taps(padded, piece.reshape(3, 3, count_rows, out_width)).astype(
        jnp.bfloat16
    )
    partial_value = lax.optimization_barrier(partial_value).astype(jnp.float32)
    width_group = activation.shape[3]
    summed = lax.psum(partial_value.astype(jnp.bfloat16), "ch").astype(jnp.float32)
    summed = lax.dynamic_slice_in_dim(summed, lax.axis_index("ch") * width_group, width_group, 3)
    return summed + bias_vec


def body(features, kernel_one, bias_one, kernel_two, bias_two):
    act_zero = jax.nn.silu(features.astype(jnp.float32)).astype(jnp.bfloat16)
    hidden = conv_sum(act_zero, kernel_one, bias_one)
    act_one = jax.nn.silu(hidden).astype(jnp.bfloat16)
    second = conv_sum(act_one, kernel_two, bias_two)
    return ((features.astype(jnp.float32) + second) * skip_scale).astype(jnp.bfloat16)


def solution(mesh):
    placed = (
        P(None, "lat", "lon", "ch"),
        P(None, None, "ch", "lon", None),
        P("ch"),
        P(None, None, "ch", "lon", None),
        P("ch"),
    )
    return jax.shard_map(
        body, mesh=mesh, in_specs=placed, out_specs=P(None, "lat", "lon", "ch"), check_vma=False
    )
```

profile of v0, /device:TPU:0, one launch (start us, length us, event | category | flops | bytes accessed | tf_op | source)
XLA Modules:
  0.0 274.4 jit_solution(6165052699699333967)
XLA Ops:
  6.5 0.7 all-gather.3.cloned.1.call-update
  7.3 0.9 fusion.7
  8.3 4.1 %collective-permute-start = (bf16[1,2,24,256]{3,2,1,0:T(8,128)(2,1)S(1)}, bf16[1,2,24,256]{3,2,1,0:T(8,128)(2,1)S(1)}, u32[]{:S(2)}, u32[]{:S(2)}) collective-permute-start(bf16[1,2,24,256]{3,2,1,0:T(8,128)(2,1)S(1)} %pad_maximum_fusion.6), channel_id=1, source_target_pairs={{8,0},{12,4},{0,8},{4,12},{9,1},{13,5},{1,9},{5,13},{10,2},{14,6},... | collective-permute-start | bytes 73736 | tf_op jit(solution)/shard_map/ppermute | solution.py:25
  12.4 3.4 %collective-permute-start.1 = (bf16[1,1,24,256]{3,2,1,0:T(8,128)(2,1)S(1)}, bf16[1,1,24,256]{3,2,1,0:T(8,128)(2,1)S(1)}, u32[]{:S(2)}, u32[]{:S(2)}) collective-permute-start(bf16[1,1,24,256]{3,2,1,0:T(8,128)(2,1)S(1)} %get-tuple-element.32), channel_id=1, source_target_pairs={{0,16},{1,17},{2,18},{3,19},{4,20},{5,21},{6,22},{7,23},{8,24},{9,... | collective-permute-start | bytes 36872 | tf_op jit(solution)/shard_map/ppermute | solution.py:16
  15.8 1.3 collective-permute-start.2
  17.2 4.2 %collective-permute-done.2 = bf16[1,1,24,256]{3,2,1,0:T(8,128)(2,1)S(1)} collective-permute-done((bf16[1,1,24,256]{3,2,1,0:T(8,128)(2,1)S(1)}, bf16[1,1,24,256]{3,2,1,0:T(8,128)(2,1)S(1)}, u32[]{:S(2)}, u32[]{:S(2)}) %collective-permute-start.2) | collective-permute-done | bytes 12320 | tf_op jit(solution)/shard_map/ppermute | solution.py:17
  21.4 1.6 collective-permute-start.3
  23.0 2.2 collective-permute-start.4
  25.3 1.8 collective-permute-done.3
  27.3 74.0 %all-gather.3.cloned.1.call-done = bf16[3,3,1,256,1024]{4,3,2,1,0:T(8,128)(2,1)} async-done(((bf16[3,3,1,64,1024]{4,3,2,1,0:T(8,128)(2,1)}), bf16[3,3,1,256,1024]{4,3,2,1,0:T(8,128)(2,1)}) %all-gather.3.cloned.1.call-update) | async-done | bytes 4718608 | tf_op jit(solution)/shard_map/all_gather | solution.py:61
  101.3 1.4 fusion.3
  102.7 1.4 convolution_add_fusion.15
  104.1 1.3 convolution_add_fusion.14
  106.3 0.3 convolution_add_fusion.10
  106.8 1.0 fusion
  107.9 0.7 all-gather.5.cloned.1.call-update
  108.6 29.9 %all-reduce.3.cloned.1.call-done = bf16[1,7,24,1024]{3,2,1,0:T(8,128)(2,1)} async-done(((bf16[1,7,24,1024]{3,2,1,0:T(8,128)(2,1)}), bf16[1,7,24,1024]{3,2,1,0:T(8,128)(2,1)}) %all-reduce.3.cloned.1.call-update) | async-done | bytes 344080 | tf_op jit(solution)/shard_map/psum | solution.py:68
  138.6 0.9 multiply_convert_fusion
  139.5 2.5 collective-permute-start.5
  142.0 3.4 %collective-permute-start.6 = (bf16[1,1,24,256]{3,2,1,0:T(8,128)(2,1)S(1)}, bf16[1,1,24,256]{3,2,1,0:T(8,128)(2,1)S(1)}, u32[]{:S(2)}, u32[]{:S(2)}) collective-permute-start(bf16[1,1,24,256]{3,2,1,0:T(8,128)(2,1)S(1)} %get-tuple-element.28), channel_id=1, source_target_pairs={{0,16},{1,17},{2,18},{3,19},{4,20},{5,21},{6,22},{7,23},{8,24},{9,... | collective-permute-start | bytes 36872 | tf_op jit(solution)/shard_map/ppermute | solution.py:16
  145.4 1.3 collective-permute-start.7
  146.8 4.2 %collective-permute-done.7 = bf16[1,1,24,256]{3,2,1,0:T(8,128)(2,1)S(1)} collective-permute-done((bf16[1,1,24,256]{3,2,1,0:T(8,128)(2,1)S(1)}, bf16[1,1,24,256]{3,2,1,0:T(8,128)(2,1)S(1)}, u32[]{:S(2)}, u32[]{:S(2)}) %collective-permute-start.7) | collective-permute-done | bytes 12320 | tf_op jit(solution)/shard_map/ppermute | solution.py:17
  151.0 1.5 collective-permute-start.8
  152.5 2.3 collective-permute-start.9
  154.9 75.1 %all-gather.5.cloned.1.call-done = bf16[3,3,1,256,1024]{4,3,2,1,0:T(8,128)(2,1)} async-done(((bf16[3,3,1,64,1024]{4,3,2,1,0:T(8,128)(2,1)}), bf16[3,3,1,256,1024]{4,3,2,1,0:T(8,128)(2,1)}) %all-gather.5.cloned.1.call-update) | async-done | bytes 4718608 | tf_op jit(solution)/shard_map/all_gather | solution.py:61
  230.0 1.4 fusion.2
  231.6 1.3 convolution_add_fusion.7
  233.8 0.3 convolution_add_fusion.3
  234.0 0.3 convolution_add_fusion.2
  234.6 1.0 fusion.1
  235.6 30.7 %all-reduce.5.cloned.1.call-done = bf16[1,7,24,1024]{3,2,1,0:T(8,128)(2,1)} async-done(((bf16[1,7,24,1024]{3,2,1,0:T(8,128)(2,1)}), bf16[1,7,24,1024]{3,2,1,0:T(8,128)(2,1)}) %all-reduce.5.cloned.1.call-update) | async-done | bytes 344080 | tf_op jit(solution)/shard_map/psum | solution.py:68
  266.3 1.6 fusion.9
  (46 shorter events, 2.7 us)
Async XLA Ops:
  6.5 94.7 %all-gather.3.cloned.1.call-start = ((), (), s32[]{:S(2)}) async-start(), calls=%async_computation | async-start | bytes 5898240 | tf_op jit(solution)/shard_map/all_gather | solution.py:61
  7.3 131.3 %all-reduce.3.cloned.1.call-start = ((), (), s32[]{:S(2)}) async-start(), calls=%async_computation.1 | async-start | bytes 688128 | tf_op jit(solution)/shard_map/psum | solution.py:68
  8.3 13.1 %collective-permute-start = (bf16[1,2,24,256]{3,2,1,0:T(8,128)(2,1)S(1)}, bf16[1,2,24,256]{3,2,1,0:T(8,128)(2,1)S(1)}, u32[]{:S(2)}, u32[]{:S(2)}) collective-permute-start(bf16[1,2,24,256]{3,2,1,0:T(8,128)(2,1)S(1)} %pad_maximum_fusion.6), channel_id=1, source_target_pairs={{8,0},{12,4},{0,8},{4,12},{9,1},{13,5},{1,9},{5,13},{10,2},{14,6},... | collective-permute-start | bytes 73736 | tf_op jit(solution)/shard_map/ppermute | solution.py:25
  12.4 4.8 %collective-permute-start.1 = (bf16[1,1,24,256]{3,2,1,0:T(8,128)(2,1)S(1)}, bf16[1,1,24,256]{3,2,1,0:T(8,128)(2,1)S(1)}, u32[]{:S(2)}, u32[]{:S(2)}) collective-permute-start(bf16[1,1,24,256]{3,2,1,0:T(8,128)(2,1)S(1)} %get-tuple-element.32), channel_id=1, source_target_pairs={{0,16},{1,17},{2,18},{3,19},{4,20},{5,21},{6,22},{7,23},{8,24},{9,... | collective-permute-start | bytes 36872 | tf_op jit(solution)/shard_map/ppermute | solution.py:16
  15.8 5.6 %collective-permute-start.2 = (bf16[1,1,24,256]{3,2,1,0:T(8,128)(2,1)S(1)}, bf16[1,1,24,256]{3,2,1,0:T(8,128)(2,1)S(1)}, u32[]{:S(2)}, u32[]{:S(2)}) collective-permute-start(bf16[1,1,24,256]{3,2,1,0:T(8,128)(2,1)S(1)} %get-tuple-element.31), channel_id=1, source_target_pairs={{16,0},{17,1},{18,2},{19,3},{20,4},{21,5},{22,6},{23,7},{24,8},{25... | collective-permute-start | bytes 36872 | tf_op jit(solution)/shard_map/ppermute | solution.py:17
  21.4 5.7 %collective-permute-start.3 = (bf16[1,9,1,256]{3,2,1,0:T(2,128)(2,1)S(1)}, bf16[1,9,1,256]{3,2,1,0:T(2,128)(2,1)S(1)}, u32[]{:S(2)}, u32[]{:S(2)}) collective-permute-start(bf16[1,9,1,256]{3,2,1,0:T(2,128)(2,1)S(1)} %get-tuple-element.24), channel_id=1, source_target_pairs={{0,4},{4,8},{8,12},{12,0},{1,5},{5,9},{9,13},{13,1},{2,6},{6,10},{... | collective-permute-start | bytes 13832 | tf_op jit(solution)/shard_map/ppermute | solution.py:16
  23.0 4.1 %collective-permute-start.4 = (bf16[1,9,1,256]{3,2,1,0:T(2,128)(2,1)S(1)}, bf16[1,9,1,256]{3,2,1,0:T(2,128)(2,1)S(1)}, u32[]{:S(2)}, u32[]{:S(2)}) collective-permute-start(bf16[1,9,1,256]{3,2,1,0:T(2,128)(2,1)S(1)} %get-tuple-element.23), channel_id=1, source_target_pairs={{4,0},{8,4},{12,8},{0,12},{5,1},{9,5},{13,9},{1,13},{6,2},{10,6},{... | collective-permute-start | bytes 13832 | tf_op jit(solution)/shard_map/ppermute | solution.py:17
  101.3 4.2 %copy-start.1 = (bf16[3,3,1,256,1024]{4,3,2,1,0:T(8,128)(2,1)S(1)}, bf16[3,3,1,256,1024]{4,3,2,1,0:T(8,128)(2,1)}, u32[]{:S(2)}) copy-start(bf16[3,3,1,256,1024]{4,3,2,1,0:T(8,128)(2,1)} %all-gather.3.cloned.1.call-done) | copy-start | bytes 14155780
  106.0 32.6 %copy-start.3 = (f32[256]{0:T(256)S(1)}, f32[256]{0:T(256)}, u32[]{:S(2)}) copy-start(f32[256]{0:T(256)} %param.7) | copy-start | bytes 3076
  107.8 122.2 %all-gather.5.cloned.1.call-start = ((), (), s32[]{:S(2)}) async-start(), calls=%async_computation.2 | async-start | bytes 5898240 | tf_op jit(solution)/shard_map/all_gather | solution.py:61
  108.6 157.7 %all-reduce.5.cloned.1.call-start = ((), (), s32[]{:S(2)}) async-start(), calls=%async_computation.3 | async-start | bytes 688128 | tf_op jit(solution)/shard_map/psum | solution.py:68
  139.5 11.4 %collective-permute-start.5 = (bf16[1,2,24,256]{3,2,1,0:T(8,128)(2,1)S(1)}, bf16[1,2,24,256]{3,2,1,0:T(8,128)(2,1)S(1)}, u32[]{:S(2)}, u32[]{:S(2)}) collective-permute-start(bf16[1,2,24,256]{3,2,1,0:T(8,128)(2,1)S(1)} %pad_maximum_fusion.7), channel_id=1, source_target_pairs={{8,0},{12,4},{0,8},{4,12},{9,1},{13,5},{1,9},{5,13},{10,2},{14,6},... | collective-permute-start | bytes 73736 | tf_op jit(solution)/shard_map/ppermute | solution.py:25
  142.0 4.8 %collective-permute-start.6 = (bf16[1,1,24,256]{3,2,1,0:T(8,128)(2,1)S(1)}, bf16[1,1,24,256]{3,2,1,0:T(8,128)(2,1)S(1)}, u32[]{:S(2)}, u32[]{:S(2)}) collective-permute-start(bf16[1,1,24,256]{3,2,1,0:T(8,128)(2,1)S(1)} %get-tuple-element.28), channel_id=1, source_target_pairs={{0,16},{1,17},{2,18},{3,19},{4,20},{5,21},{6,22},{7,23},{8,24},{9,... | collective-permute-start | bytes 36872 | tf_op jit(solution)/shard_map/ppermute | solution.py:16
  145.4 5.6 %collective-permute-start.7 = (bf16[1,1,24,256]{3,2,1,0:T(8,128)(2,1)S(1)}, bf16[1,1,24,256]{3,2,1,0:T(8,128)(2,1)S(1)}, u32[]{:S(2)}, u32[]{:S(2)}) collective-permute-start(bf16[1,1,24,256]{3,2,1,0:T(8,128)(2,1)S(1)} %get-tuple-element.27), channel_id=1, source_target_pairs={{16,0},{17,1},{18,2},{19,3},{20,4},{21,5},{22,6},{23,7},{24,8},{25... | collective-permute-start | bytes 36872 | tf_op jit(solution)/shard_map/ppermute | solution.py:17
  151.0 80.5 %collective-permute-start.8 = (bf16[1,9,1,256]{3,2,1,0:T(2,128)(2,1)S(1)}, bf16[1,9,1,256]{3,2,1,0:T(2,128)(2,1)S(1)}, u32[]{:S(2)}, u32[]{:S(2)}) collective-permute-start(bf16[1,9,1,256]{3,2,1,0:T(2,128)(2,1)S(1)} %get-tuple-element.20), channel_id=1, source_target_pairs={{0,4},{4,8},{8,12},{12,0},{1,5},{5,9},{9,13},{13,1},{2,6},{6,10},{... | collective-permute-start | bytes 13832 | tf_op jit(solution)/shard_map/ppermute | solution.py:16
  152.5 78.9 %collective-permute-start.9 = (bf16[1,9,1,256]{3,2,1,0:T(2,128)(2,1)S(1)}, bf16[1,9,1,256]{3,2,1,0:T(2,128)(2,1)S(1)}, u32[]{:S(2)}, u32[]{:S(2)}) collective-permute-start(bf16[1,9,1,256]{3,2,1,0:T(2,128)(2,1)S(1)} %get-tuple-element.19), channel_id=1, source_target_pairs={{4,0},{8,4},{12,8},{0,12},{5,1},{9,5},{13,9},{1,13},{6,2},{10,6},{... | collective-permute-start | bytes 13832 | tf_op jit(solution)/shard_map/ppermute | solution.py:17
  230.0 2.9 %copy-start = (bf16[3,3,1,256,1024]{4,3,2,1,0:T(8,128)(2,1)S(1)}, bf16[3,3,1,256,1024]{4,3,2,1,0:T(8,128)(2,1)}, u32[]{:S(2)}) copy-start(bf16[3,3,1,256,1024]{4,3,2,1,0:T(8,128)(2,1)} %all-gather.5.cloned.1.call-done) | copy-start | bytes 14155780
  233.5 32.8 %copy-start.2 = (bf16[1,7,24,256]{3,2,1,0:T(8,128)(2,1)S(1)}, bf16[1,7,24,256]{3,2,1,0:T(8,128)(2,1)}, u32[]{:S(2)}) copy-start(bf16[1,7,24,256]{3,2,1,0:T(8,128)(2,1)} %param.5) | copy-start | bytes 258052
  233.5 32.8 %copy-start.4 = (f32[256]{0:T(256)S(1)}, f32[256]{0:T(256)}, u32[]{:S(2)}) copy-start(f32[256]{0:T(256)} %param.9) | copy-start | bytes 3076
Sparse Core Ops, SparseCore 0:
  8.9 92.2 all-gather.2
  108.0 30.5 all-reduce.2
  140.1 89.8 all-gather.4
  235.7 30.5 all-reduce.4
where the time goes:
time: 275 us; the launch traced here: 274 us
  waiting for transfers between devices  222 us (81%)
  starting transfers between devices  23.8 us (9%)
  between operations  13.5 us (5%)
  matrix products  11.8 us (4%)
  other arithmetic  3.66 us (1%)
    all_gather x2, waiting for transfers between devices, conv_sum(): piece = lax.all_gather(kernel, 'lon', axis=3, tiled=True)  149 us
    psum x2, waiting for transfers between devices, conv_sum(): lax.psum(partial_value.astype(jnp.bfloat16), 'ch').astype(jnp.float32)  60.7 us
    dot_general x18, matrix products, apply_taps(): jnp.dot(window, kernel[row_off, col_off], preferred_element_type=jnp.floa...  11.8 us
    ppermute x4, starting transfers between devices, extended(): before = lax.ppermute(last, axis, up)  9.91 us
    ppermute x4, waiting for transfers between devices, extended(): after = lax.ppermute(leading, axis, down)  8.41 us
    ppermute x4, starting transfers between devices, extended(): after = lax.ppermute(leading, axis, down)  7.17 us
    ppermute x2, starting transfers between devices, shifted(): return lax.ppermute(block, axis, route)  6.57 us
  transfers between devices with their start and end apart: 14, of which 9 were waited for; matrix products, arithmetic and copies ran while one was open for 1% of the time, Pallas kernels for 0%

commit v1 on v0

v1 whole, which is shorter than its diff:
```python
import functools

import jax
import jax.numpy as jnp
from jax import lax
from jax.experimental import pallas as pl
from jax.experimental.pallas import tpu as pltpu
from jax.sharding import PartitionSpec as P

skip_scale = 0.7071067811865476
MESH = pl.DeviceIdType.MESH
EDGE = 8


def round_up(value, step):
    return -(-value // step) * step


def silu(value):
    return value / (1.0 + jnp.exp(-value))


def block_kernel(
    n_lat, n_lon, x_ref, k1_ref, b1_ref, k2_ref, b2_ref, out_ref,
    w, apack, arecv, hpack, hrecv, field, taps, acc, ysend, yrecv, zsend, zrecv,
    wl_sem, ws_sem, wr_sem, as_sem, ar_sem, hs_sem, hr_sem, ys_sem, yr_sem, zs_sem, zr_sem,
):
    rows, cols, width = x_ref.shape[1:]
    cells = rows * cols
    part = width // n_lon
    half = apack.shape[2]
    all_cols = cols * n_lon
    lat, lon, ch = lax.axis_index("lat"), lax.axis_index("lon"), lax.axis_index("ch")
    near = ch + 1 - 2 * (ch % 2)
    far = ch + 2 - 4 * ((ch // 2) % 2)
    near_far = near + 2 - 4 * ((near // 2) % 2)
    order = list(range(1, n_lon)) + [0]

    def device(up, along, channel):
        return {"lat": (lat + up) % n_lat, "lon": (lon + along) % n_lon, "ch": channel}

    def remote(src, dst, send, recv, target):
        return pltpu.make_async_remote_copy(
            src_ref=src, dst_ref=dst, send_sem=send, recv_sem=recv,
            device_id=target, device_id_type=MESH,
        )

    def weight_copies(conv, slot):
        source = (k1_ref, k2_ref)[conv]
        mine, theirs = ((ch, near), (far, near_far))[slot]

        def outputs(group):
            return source.at[:, :, 0, :, pl.ds(pl.multiple_of(group * width, width), width)]

        return (
            pltpu.make_async_copy(outputs(mine), w.at[conv, slot, :, :, 0], wl_sem.at[conv, slot]),
            remote(
                outputs(theirs), w.at[conv, slot, :, :, 1],
                ws_sem.at[conv, slot], wr_sem.at[conv, slot], device(0, 0, near),
            ),
        )

    weights = {(conv, slot): weight_copies(conv, slot) for conv in (0, 1) for slot in (1, 0)}
    for local, _ in weights.values():
        local.start()

    barrier = pltpu.get_barrier_semaphore()
    greeted = 0
    for up in sorted({0, 1, n_lat - 1}):
        for along in range(n_lon):
            for channel in (ch, near):
                if up == 0 and along == 0 and channel is ch:
                    continue
                pl.semaphore_signal(barrier, inc=1, device_id=device(up, along, channel), device_id_type=MESH)
                greeted += 1
    pl.semaphore_signal(barrier, inc=1, device_id=device(0, 0, far), device_id_type=MESH)
    pl.semaphore_wait(barrier, greeted + 1)
    for slot in (1, 0):
        weights[0, slot][1].start()

    def pack(act, conv):
        for j in range(n_lon):
            piece = act[:, j * part:(j + 1) * part]
            lower = jnp.concatenate(
                [piece[half:], jnp.zeros((2 * half - cells, part), jnp.float32)], axis=0
            )
            apack[conv, j] = jnp.concatenate([piece[:half], lower], axis=1).astype(jnp.bfloat16)
            fill = jnp.zeros((hpack.shape[3] - cols, part), jnp.float32)
            hpack[conv, 0, j] = jnp.concatenate([piece[cells - cols:], fill], axis=0).astype(jnp.bfloat16)
            hpack[conv, 1, j] = jnp.concatenate([piece[:cols], fill], axis=0).astype(jnp.bfloat16)

    def unpack(block):
        block = block.astype(jnp.float32)
        whole = jnp.concatenate([block[:, :part], block[:cells - half, part:]], axis=0)
        return whole.reshape(rows, cols, part)

    def main_copy(conv, p, k):
        return remote(
            apack.at[conv, (lon + k) % n_lon], arecv.at[conv, p, k],
            as_sem.at[conv, p, k], ar_sem.at[conv, p, k], device(0, k, (ch, near)[p]),
        )

    def halo_copy(conv, side, p, k):
        return remote(
            hpack.at[conv, side, (lon + k) % n_lon], hrecv.at[conv, side, p, k],
            hs_sem.at[conv, side, p, k], hr_sem.at[conv, side, p, k],
            device((1, -1)[side] % n_lat, k, (ch, near)[p]),
        )

    mains = [(p, k) for k in order for p in (0, 1) if (p, k) != (0, 0)]
    halos = [(p, k) for k in order for p in (0, 1)]
    sends = (lat < n_lat - 1, lat > 0)
    gets = (lat > 0, lat < n_lat - 1)

    def exchange(conv):
        for p, k in mains:
            main_copy(conv, p, k).start()
        for side in (0, 1):
            @pl.when(sends[side])
            def _():
                for p, k in halos:
                    halo_copy(conv, side, p, k).start()

    def assemble(conv):
        def place(k):
            return pl.ds(pl.multiple_of(EDGE + ((lon - k + n_lon) % n_lon) * cols, 8), cols)

        def lanes(p):
            return slice(p * part, (p + 1) * part)

        field[1:rows + 1, place(0), lanes(0)] = unpack(apack[conv, lon])
        for p, k in mains:
            main_copy(conv, p, k).wait_recv()
            field[1:rows + 1, place(k), lanes(p)] = unpack(arecv[conv, p, k])
        for side in (0, 1):
            row, inner = ((0, 1), (rows + 1, rows))[side]

            @pl.when(gets[side])
            def _():
                for p, k in halos:
                    halo_copy(conv, side, p, k).wait_recv()
                    field[row, place(k), lanes(p)] = hrecv[conv, side, p, k].astype(jnp.float32)[:cols]

            @pl.when(jnp.logical_not(gets[side]))
            def _():
                turn = all_cols // 2
                field[row, EDGE:EDGE + turn] = field[inner, EDGE + turn:EDGE + all_cols]
                field[row, EDGE + turn:EDGE + all_cols] = field[inner, EDGE:EDGE + turn]

        field[:, EDGE - 1:EDGE] = field[:, EDGE + all_cols - 1:EDGE + all_cols]
        field[:, EDGE + all_cols:EDGE + all_cols + 1] = field[:, EDGE:EDGE + 1]
        for e in range(3):
            taps[:, :, e * 2 * part:(e + 1) * 2 * part] = field[
                :, EDGE - 1 + e:EDGE - 1 + e + all_cols
            ].astype(jnp.bfloat16)

    def multiply(conv, slot):
        local, other = weights[conv, slot]
        local.wait()
        other.wait_recv()
        total = None
        for a in range(3):
            term = jnp.dot(
                taps[a:a + rows].reshape(rows * all_cols, 6 * part),
                w[conv, slot, a].reshape(6 * part, width),
                preferred_element_type=jnp.float32,
            )
            total = term if total is None else total + term
        acc[slot] = total.reshape(rows, all_cols, width)

    def chunk(slot, k):
        start = pl.multiple_of(((lon + k) % n_lon) * cols, 8)
        return acc[slot, :, pl.ds(start, cols), :].reshape(cells, width)

    def padded(value):
        fill = jnp.zeros((ysend.shape[2] - cells, width), jnp.float32)
        return jnp.concatenate([value, fill], axis=0).astype(jnp.bfloat16)

    def far_copy(conv, k):
        return remote(
            ysend.at[conv, k], yrecv.at[conv, k], ys_sem.at[conv, k], yr_sem.at[conv, k],
            device(0, 0, far),
        )

    def along_copy(conv, k):
        return remote(
            zsend.at[conv, k], zrecv.at[conv, k], zs_sem.at[conv, k], zr_sem.at[conv, k],
            device(0, k, ch),
        )

    def conv_sum(conv, bias):
        assemble(conv)
        multiply(conv, 1)
        for k in order:
            ysend[conv, k] = padded(chunk(1, k))
            far_copy(conv, k).start()
        multiply(conv, 0)
        total = None
        for k in order:
            far_copy(conv, k).wait_recv()
            value = chunk(0, k) + yrecv[conv, k].astype(jnp.float32)[:cells]
            if k:
                zsend[conv, k] = padded(value)
                along_copy(conv, k).start()
            else:
                total = value
        for k in order[:-1]:
            along_copy(conv, k).wait_recv()
            total = total + zrecv[conv, k].astype(jnp.float32)[:cells]
        return total + bias

    features = x_ref[0].astype(jnp.float32).reshape(cells, width)
    pack(silu(features), 0)
    exchange(0)
    for slot in (1, 0):
        weights[1, slot][1].start()
    hidden = conv_sum(0, b1_ref[...])
    pack(silu(hidden), 1)
    exchange(1)
    second = conv_sum(1, b2_ref[...])
    features = x_ref[0].astype(jnp.float32).reshape(cells, width)
    result = (features + second) * skip_scale
    out_ref[0] = result.reshape(rows, cols, width).astype(jnp.bfloat16)

    for conv in (0, 1):
        for slot in (0, 1):
            weights[conv, slot][1].wait_send()
        for p, k in mains:
            main_copy(conv, p, k).wait_send()
        for side in (0, 1):
            @pl.when(sends[side])
            def _():
                for p, k in halos:
                    halo_copy(conv, side, p, k).wait_send()
        for k in order:
            far_copy(conv, k).wait_send()
            if k:
                along_copy(conv, k).wait_send()


def body(n_lat, n_lon, features, kernel_one, bias_one, kernel_two, bias_two):
    _, rows, cols, width = features.shape
    cells, part, all_cols = rows * cols, width // n_lon, cols * n_lon
    half = round_up(-(-cells // 2), 16)
    tall = round_up(cells, 16)
    bf16, f32 = jnp.bfloat16, jnp.float32
    dma = pltpu.SemaphoreType.DMA
    vmem = pl.BlockSpec(memory_space=pltpu.VMEM)
    anywhere = pl.BlockSpec(memory_space=pl.ANY)
    return pl.pallas_call(
        functools.partial(block_kernel, n_lat, n_lon),
        out_shape=jax.ShapeDtypeStruct(features.shape, bf16),
        in_specs=[vmem, anywhere, vmem, anywhere, vmem],
        out_specs=vmem,
        scratch_shapes=[
            pltpu.VMEM((2, 2, 3, 3, 2, part, width), bf16),
            pltpu.VMEM((2, n_lon, half, 2 * part), bf16),
            pltpu.VMEM((2, 2, n_lon, half, 2 * part), bf16),
            pltpu.VMEM((2, 2, n_lon, round_up(cols, 16), part), bf16),
            pltpu.VMEM((2, 2, 2, n_lon, round_up(cols, 16), part), bf16),
            pltpu.VMEM((rows + 2, all_cols + 2 * EDGE, 2 * part), f32),
            pltpu.VMEM((rows + 2, all_cols, 6 * part), bf16),
            pltpu.VMEM((2, rows, all_cols, width), f32),
            pltpu.VMEM((2, n_lon, tall, width), bf16),
            pltpu.VMEM((2, n_lon, tall, width), bf16),
            pltpu.VMEM((2, n_lon, tall, width), bf16),
            pltpu.VMEM((2, n_lon, tall, width), bf16),
            dma((2, 2)), dma((2, 2)), dma((2, 2)),
            dma((2, 2, n_lon)), dma((2, 2, n_lon)),
            dma((2, 2, 2, n_lon)), dma((2, 2, 2, n_lon)),
            dma((2, n_lon)), dma((2, n_lon)), dma((2, n_lon)), dma((2, n_lon)),
        ],
        compiler_params=pltpu.CompilerParams(
            collective_id=0, has_side_effects=True, vmem_limit_bytes=56 * 2**20
        ),
        name="residual_block",
    )(features, kernel_one, bias_one.reshape(1, width), kernel_two, bias_two.reshape(1, width))


def solution(mesh):
    placed = (
        P(None, "lat", "lon", "ch"),
        P(None, None, "ch", "lon", None),
        P("ch"),
        P(None, None, "ch", "lon", None),
        P("ch"),
    )
    return jax.shard_map(
        functools.partial(body, mesh.shape["lat"], mesh.shape["lon"]),
        mesh=mesh, in_specs=placed, out_specs=P(None, "lat", "lon", "ch"), check_vma=False,
    )
```

time: 275 us -> 55.8 us (0.20)
  waiting for transfers between devices: 222 us -> 0 us
  Pallas kernels: 0 us -> 54.1 us
  starting transfers between devices: 23.8 us -> 0 us
  between operations: 13.5 us -> 0.01 us
  matrix products: 11.8 us -> 0 us
  other arithmetic: 3.66 us -> 0 us
    all_gather x2 -> x0, waiting for transfers between devices: 149 us -> none  [conv_sum(): piece = lax.all_gather(kernel, 'lon', axis=3, tiled=True)]
    psum x2 -> x0, waiting for transfers between devices: 60.7 us -> none  [conv_sum(): lax.psum(partial_value.astype(jnp.bfloat16), 'ch').astype(jnp.float32)]
    pallas_call x0 -> x1, Pallas kernels: none -> 54.1 us  [body(): pl.pallas_call(functools.partial(block_kernel, n_lat, n_lon), out_shape=j...]
    ppermute x10 -> x0, starting transfers between devices: 23.7 us -> none  [the longest x4 9.91 us: extended(): before = lax.ppermute(last, axis, up)]
    dot_general x18 -> x0, matrix products: 11.8 us -> none  [apply_taps(): jnp.dot(window, kernel[row_off, col_off], preferred_element_type=jnp.floa...]
    ppermute x10 -> x0, waiting for transfers between devices: 10.4 us -> none  [the longest x4 8.41 us: extended(): after = lax.ppermute(leading, axis, down)]
    convert_element_type x3 -> x0, other arithmetic: 3.45 us -> none  [the longest x1 1.56 us: body(): ((features.astype(jnp.float32) + second) * skip_scale).astype(jnp.bfloat16)]
  transfers between devices with their start and end apart: 14 -> 0, of which waited for: 9 -> 0; matrix products, arithmetic and copies ran while one was open for 1% -> 0% of each run, Pallas kernels for 0% -> 0%
where the time goes in v1:
time: 55.8 us; the launch traced here: 55.6 us
  Pallas kernels  54.1 us (97%)
  local copies, waits for them, and re-layouts  1.53 us (3%)
    pallas_call x1, Pallas kernels, body(): pl.pallas_call(functools.partial(block_kernel, n_lat, n_lon), out_shape=j...  54.1 us
    unnamed x1, local copies, waits for them, and re-layouts  1.53 us

profile of v1, /device:TPU:0, one launch (start us, length us, event | category | flops | bytes accessed | tf_op | source)
XLA Modules:
  0.0 55.6 jit_solution(7254293586733194761)
XLA Ops:
  0.0 54.1 %residual_block.1 = bf16[1,7,24,256]{3,2,1,0:T(8,128)(2,1)} custom-call(bf16[1,7,24,256]{3,2,1,0:T(8,128)(2,1)} %x_ref.1, bf16[3,3,1,64,1024]{4,3,2,1,0:T(8,128)(2,1)} %k1_ref.1, f32[1,256]{1,0:T(1,128)} %bitcast.2, bf16[3,3,1,64,1024]{4,3,2,1,0:T(8,128)(2,1)} %k2_ref.1, f32[1,256]{1,0:T(1,128)} %bitcast.3), custom_call_target="tpu_custom_call" | custom-call | tf_op jit(solution)/shard_map/residual_block/pallas_call | solution.py:250
  54.1 1.5 %copy.7 = bf16[1,7,24,256]{3,2,1,0:T(8,128)(2,1)} copy(bf16[1,7,24,256]{3,2,1,0:T(8,128)(2,1)} %residual_block.1) | data formatting | bytes 172032

commit v2 on v1

--- a/solution.py
+++ b/solution.py
@@ -23,7 +23,7 @@
 def block_kernel(
     n_lat, n_lon, x_ref, k1_ref, b1_ref, k2_ref, b2_ref, out_ref,
     w, apack, arecv, hpack, hrecv, field, taps, acc, ysend, yrecv, zsend, zrecv,
-    wl_sem, ws_sem, wr_sem, as_sem, ar_sem, hs_sem, hr_sem, ys_sem, yr_sem, zs_sem, zr_sem,
+    wl_sem, ws_sem, wr_sem, as_sem, ar_sem, hs_sem, hr_sem, fs_sem, fr_sem, ys_sem, yr_sem, zs_sem, zr_sem,
 ):
     rows, cols, width = x_ref.shape[1:]
     cells = rows * cols
@@ -66,17 +66,10 @@
 
     barrier = pltpu.get_barrier_semaphore()
     greeted = 0
-    for up in sorted({0, 1, n_lat - 1}):
-        for along in range(n_lon):
-            for channel in (ch, near):
-                if up == 0 and along == 0 and channel is ch:
-                    continue
-                pl.semaphore_signal(barrier, inc=1, device_id=device(up, along, channel), device_id_type=MESH)
-                greeted += 1
-    pl.semaphore_signal(barrier, inc=1, device_id=device(0, 0, far), device_id_type=MESH)
-    pl.semaphore_wait(barrier, greeted + 1)
-    for slot in (1, 0):
-        weights[0, slot][1].start()
+    peers = [(up, along, ch) for up in sorted({0, 1, n_lat - 1}) for along in range(n_lon) if up or along]
+    for peer in peers + [(0, 0, near), (0, 0, far)]:
+        pl.semaphore_signal(barrier, inc=1, device_id=device(*peer), device_id_type=MESH)
+        greeted += 1
 
     def pack(act, conv):
         for j in range(n_lon):
@@ -94,32 +87,43 @@
         whole = jnp.concatenate([block[:, :part], block[:cells - half, part:]], axis=0)
         return whole.reshape(rows, cols, part)
 
-    def main_copy(conv, p, k):
-        return remote(
-            apack.at[conv, (lon + k) % n_lon], arecv.at[conv, p, k],
-            as_sem.at[conv, p, k], ar_sem.at[conv, p, k], device(0, k, (ch, near)[p]),
-        )
-
-    def halo_copy(conv, side, p, k):
-        return remote(
-            hpack.at[conv, side, (lon + k) % n_lon], hrecv.at[conv, side, p, k],
-            hs_sem.at[conv, side, p, k], hr_sem.at[conv, side, p, k],
-            device((1, -1)[side] % n_lat, k, (ch, near)[p]),
-        )
-
-    mains = [(p, k) for k in order for p in (0, 1) if (p, k) != (0, 0)]
-    halos = [(p, k) for k in order for p in (0, 1)]
+    def main_copy(conv, k):
+        return remote(
+            apack.at[conv, (lon + k) % n_lon], arecv.at[conv, 0, k],
+            as_sem.at[conv, 0, k], ar_sem.at[conv, 0, k], device(0, k, ch),
+        )
+
+    def forward_copy(conv, k):
+        return remote(
+            arecv.at[conv, 0, k] if k else apack.at[conv, lon], arecv.at[conv, 1, k],
+            as_sem.at[conv, 1, k], ar_sem.at[conv, 1, k], device(0, 0, near),
+        )
+
+    def halo_copy(conv, side, k):
+        return remote(
+            hpack.at[conv, side, (lon + k) % n_lon], hrecv.at[conv, side, 0, k],
+            hs_sem.at[conv, side, k], hr_sem.at[conv, side, k],
+            device((1, -1)[side] % n_lat, k, ch),
+        )
+
+    def halo_forward(conv, side):
+        return remote(
+            hrecv.at[conv, side, 0], hrecv.at[conv, side, 1],
+            fs_sem.at[conv, side], fr_sem.at[conv, side], device(0, 0, near),
+        )
+
     sends = (lat < n_lat - 1, lat > 0)
     gets = (lat > 0, lat < n_lat - 1)
 
     def exchange(conv):
-        for p, k in mains:
-            main_copy(conv, p, k).start()
+        for k in order[:-1]:
+            main_copy(conv, k).start()
         for side in (0, 1):
             @pl.when(sends[side])
             def _():
-                for p, k in halos:
-                    halo_copy(conv, side, p, k).start()
+                for k in order:
+                    halo_copy(conv, side, k).start()
+        forward_copy(conv, 0).start()
 
     def assemble(conv):
         def place(k):
@@ -129,17 +133,28 @@
             return slice(p * part, (p + 1) * part)
 
         field[1:rows + 1, place(0), lanes(0)] = unpack(apack[conv, lon])
-        for p, k in mains:
-            main_copy(conv, p, k).wait_recv()
-            field[1:rows + 1, place(k), lanes(p)] = unpack(arecv[conv, p, k])
+        for k in order[:-1]:
+            main_copy(conv, k).wait_recv()
+            forward_copy(conv, k).start()
+            field[1:rows + 1, place(k), lanes(0)] = unpack(arecv[conv, 0, k])
+        for side in (0, 1):
+            @pl.when(gets[side])
+            def _():
+                for k in order:
+                    halo_copy(conv, side, k).wait_recv()
+                halo_forward(conv, side).start()
+        for k in [0] + order[:-1]:
+            forward_copy(conv, k).wait_recv()
+            field[1:rows + 1, place(k), lanes(1)] = unpack(arecv[conv, 1, k])
         for side in (0, 1):
             row, inner = ((0, 1), (rows + 1, rows))[side]
 
             @pl.when(gets[side])
             def _():
-                for p, k in halos:
-                    halo_copy(conv, side, p, k).wait_recv()
-                    field[row, place(k), lanes(p)] = hrecv[conv, side, p, k].astype(jnp.float32)[:cols]
+                halo_forward(conv, side).wait_recv()
+                for p in (0, 1):
+                    for k in order:
+                        field[row, place(k), lanes(p)] = hrecv[conv, side, p, k].astype(jnp.float32)[:cols]
 
             @pl.when(jnp.logical_not(gets[side]))
             def _():
@@ -195,6 +210,9 @@
             ysend[conv, k] = padded(chunk(1, k))
             far_copy(conv, k).start()
         multiply(conv, 0)
+        if conv == 0:
+            for slot in (1, 0):
+                weights[1, slot][1].start()
         total = None
         for k in order:
             far_copy(conv, k).wait_recv()
@@ -211,9 +229,10 @@
 
     features = x_ref[0].astype(jnp.float32).reshape(cells, width)
     pack(silu(features), 0)
+    pl.semaphore_wait(barrier, greeted)
+    for slot in (1, 0):
+        weights[0, slot][1].start()
     exchange(0)
-    for slot in (1, 0):
-        weights[1, slot][1].start()
     hidden = conv_sum(0, b1_ref[...])
     pack(silu(hidden), 1)
     exchange(1)
@@ -225,13 +244,19 @@
     for conv in (0, 1):
         for slot in (0, 1):
             weights[conv, slot][1].wait_send()
-        for p, k in mains:
-            main_copy(conv, p, k).wait_send()
+        for k in order:
+            forward_copy(conv, k).wait_send()
+            if k:
+                main_copy(conv, k).wait_send()
         for side in (0, 1):
             @pl.when(sends[side])
             def _():
-                for p, k in halos:
-                    halo_copy(conv, side, p, k).wait_send()
+                for k in order:
+                    halo_copy(conv, side, k).wait_send()
+
+            @pl.when(gets[side])
+            def _():
+                halo_forward(conv, side).wait_send()
         for k in order:
             far_copy(conv, k).wait_send()
             if k:
@@ -267,7 +292,7 @@
             pltpu.VMEM((2, n_lon, tall, width), bf16),
             dma((2, 2)), dma((2, 2)), dma((2, 2)),
             dma((2, 2, n_lon)), dma((2, 2, n_lon)),
-            dma((2, 2, 2, n_lon)), dma((2, 2, 2, n_lon)),
+            dma((2, 2, n_lon)), dma((2, 2, n_lon)), dma((2, 2)), dma((2, 2)),
             dma((2, n_lon)), dma((2, n_lon)), dma((2, n_lon)), dma((2, n_lon)),
         ],
         compiler_params=pltpu.CompilerParams(

time: 55.8 us -> 52.3 us (0.937)
  Pallas kernels: 54.1 us -> 50.6 us
    pallas_call x1, Pallas kernels: 54.1 us -> 50.6 us  [body(): pl.pallas_call(functools.partial(block_kernel, n_lat, n_lon), out_shape=j...]
where the time goes in v2:
time: 52.3 us; the launch traced here: 52.1 us
  Pallas kernels  50.6 us (97%)
  local copies, waits for them, and re-layouts  1.53 us (3%)
    pallas_call x1, Pallas kernels, body(): pl.pallas_call(functools.partial(block_kernel, n_lat, n_lon), out_shape=j...  50.6 us
    unnamed x1, local copies, waits for them, and re-layouts  1.53 us

profile of v2, /device:TPU:0, one launch (start us, length us, event | category | flops | bytes accessed | tf_op | source)
XLA Modules:
  0.0 52.1 jit_solution(12520549593900128427)
XLA Ops:
  0.0 50.6 %residual_block.1 = bf16[1,7,24,256]{3,2,1,0:T(8,128)(2,1)} custom-call(bf16[1,7,24,256]{3,2,1,0:T(8,128)(2,1)} %x_ref.1, bf16[3,3,1,64,1024]{4,3,2,1,0:T(8,128)(2,1)} %k1_ref.1, f32[1,256]{1,0:T(1,128)} %bitcast.2, bf16[3,3,1,64,1024]{4,3,2,1,0:T(8,128)(2,1)} %k2_ref.1, f32[1,256]{1,0:T(1,128)} %bitcast.3), custom_call_target="tpu_custom_call" | custom-call | tf_op jit(solution)/shard_map/residual_block/pallas_call | solution.py:275
  50.6 1.5 %copy.7 = bf16[1,7,24,256]{3,2,1,0:T(8,128)(2,1)} copy(bf16[1,7,24,256]{3,2,1,0:T(8,128)(2,1)} %residual_block.1) | data formatting | bytes 172032

commit v3 on v1

v3 whole, which is shorter than its diff:
```python
import functools

import jax
import jax.numpy as jnp
from jax import lax
from jax.experimental import pallas as pl
from jax.experimental.pallas import tpu as pltpu
from jax.sharding import PartitionSpec as P

skip_scale = 0.7071067811865476
MESH = pl.DeviceIdType.MESH
EDGE = 8


def round_up(value, step):
    return -(-value // step) * step


def silu(value):
    return value / (1.0 + jnp.exp(-value))


def pack(value, half):
    count, part = value.shape
    lower = value[half:]
    if 2 * half > count:
        lower = jnp.concatenate([lower, jnp.zeros((2 * half - count, part), value.dtype)], axis=0)
    return jnp.concatenate([value[:half], lower], axis=1)


def unpack(block, count):
    half, part = block.shape[0], block.shape[1] // 2
    return jnp.concatenate([block[:, :part], block[:count - half, part:]], axis=0)


def block_kernel(
    n_lat, n_lon, x_ref, k1_ref, b1_ref, k2_ref, b2_ref, out_ref,
    w, apack, arecv, hpack, hrecv, bpack, brecv, epack, erecv, field, taps,
    own, ysend1, yrecv1, zsend1, zrecv1, acc, ysend2, yrecv2, zsend2, zrecv2,
    wl_sem, ws_sem, wr_sem, as_sem, ar_sem, hs_sem, hr_sem, fs_sem, fr_sem,
    bs_sem, br_sem, es_sem, er_sem, ys_sem, yr_sem, zs_sem, zr_sem,
):
    rows, cols, width = x_ref.shape[1:]
    cells = rows * cols
    part = width // n_lon
    half = apack.shape[1]
    all_cols = cols * n_lon
    all_cells = rows * all_cols
    band_half = bpack.shape[0]
    f32, bf16 = jnp.float32, jnp.bfloat16
    lat, lon, ch = lax.axis_index("lat"), lax.axis_index("lon"), lax.axis_index("ch")
    near = ch + 1 - 2 * (ch % 2)
    far = ch + 2 - 4 * ((ch // 2) % 2)
    near_far = near + 2 - 4 * ((near // 2) % 2)
    away = list(range(1, n_lon))
    order = away + [0]

    def device(up, along, channel):
        return {"lat": (lat + up) % n_lat, "lon": (lon + along) % n_lon, "ch": channel}

    def remote(src, dst, send, recv, target):
        return pltpu.make_async_remote_copy(
            src_ref=src, dst_ref=dst, send_sem=send, recv_sem=recv,
            device_id=target, device_id_type=MESH,
        )

    def weight_copies(conv, slot):
        source = (k1_ref, k2_ref)[conv]
        mine, theirs = ((ch, near), (far, near_far))[slot]

        def outputs(group):
            return source.at[:, :, 0, :, pl.ds(pl.multiple_of(group * width, width), width)]

        return (
            pltpu.make_async_copy(outputs(mine), w.at[conv, slot, :, :, 0], wl_sem.at[conv, slot]),
            remote(
                outputs(theirs), w.at[conv, slot, :, :, 1],
                ws_sem.at[conv, slot], wr_sem.at[conv, slot], device(0, 0, near),
            ),
        )

    weights = {(conv, slot): weight_copies(conv, slot) for conv in (0, 1) for slot in (1, 0)}
    for local, _ in weights.values():
        local.start()

    barrier = pltpu.get_barrier_semaphore()
    greeted = 0
    ups = sorted({0, 1, n_lat - 1})
    peers = [(up, along, ch) for up in ups for along in range(n_lon) if up or along]
    peers += [(up, 0, near) for up in ups] + [(0, 0, far)]
    for peer in peers:
        pl.semaphore_signal(barrier, inc=1, device_id=device(*peer), device_id_type=MESH)
        greeted += 1

    sends = (lat < n_lat - 1, lat > 0)
    gets = (lat > 0, lat < n_lat - 1)

    def main_copy(k):
        return remote(
            apack.at[(lon + k) % n_lon], arecv.at[0, k], as_sem.at[0, k], ar_sem.at[0, k], device(0, k, ch)
        )

    def forward_copy(k):
        return remote(
            arecv.at[0, k] if k else apack.at[lon], arecv.at[1, k],
            as_sem.at[1, k], ar_sem.at[1, k], device(0, 0, near),
        )

    def halo_copy(side, k):
        return remote(
            hpack.at[side, (lon + k) % n_lon], hrecv.at[side, 0, k],
            hs_sem.at[side, k], hr_sem.at[side, k], device((1, -1)[side] % n_lat, k, ch),
        )

    def halo_forward(side):
        return remote(
            hrecv.at[side, 0], hrecv.at[side, 1], fs_sem.at[side], fr_sem.at[side], device(0, 0, near)
        )

    def band_copy():
        return remote(bpack, brecv, bs_sem, br_sem, device(0, 0, near))

    def edge_copy(side, p):
        return remote(
            epack.at[side], erecv.at[side, p], es_sem.at[side, p], er_sem.at[side, p],
            device((1, -1)[side] % n_lat, 0, (ch, near)[p]),
        )

    def far_copy(conv, k):
        src, dst = ((ysend1, yrecv1), (ysend2, yrecv2))[conv]
        slot = (lon + k) % n_lon
        return remote(src.at[slot], dst.at[slot], ys_sem.at[conv, k], yr_sem.at[conv, k], device(0, 0, far))

    def along_copy(conv, k):
        src, dst = ((zsend1, zrecv1), (zsend2, zrecv2))[conv]
        return remote(src.at[k], dst.at[k], zs_sem.at[conv, k], zr_sem.at[conv, k], device(0, k, ch))

    def lanes(p):
        return slice(p * part, (p + 1) * part)

    inside = slice(EDGE, EDGE + all_cols)

    def fold(side):
        row, inner = ((0, 1), (rows + 1, rows))[side]
        turn = all_cols // 2
        field[row, EDGE:EDGE + turn] = field[inner, EDGE + turn:EDGE + all_cols]
        field[row, EDGE + turn:EDGE + all_cols] = field[inner, EDGE:EDGE + turn]

    def spread():
        field[:, EDGE - 1:EDGE] = field[:, EDGE + all_cols - 1:EDGE + all_cols]
        field[:, EDGE + all_cols:EDGE + all_cols + 1] = field[:, EDGE:EDGE + 1]
        for e in range(3):
            taps[:, :, e * 2 * part:(e + 1) * 2 * part] = field[
                :, EDGE - 1 + e:EDGE - 1 + e + all_cols
            ].astype(bf16)

    def exchange_one():
        for k in away:
            main_copy(k).start()
        for side in (0, 1):
            @pl.when(sends[side])
            def _():
                for k in order:
                    halo_copy(side, k).start()
        forward_copy(0).start()

    def assemble_one():
        def place(k):
            return pl.ds(pl.multiple_of(EDGE + ((lon - k + n_lon) % n_lon) * cols, 8), cols)

        def cell_block(block):
            return unpack(block.astype(f32), cells).reshape(rows, cols, part)

        field[1:rows + 1, place(0), lanes(0)] = cell_block(apack[lon])
        for k in away:
            main_copy(k).wait_recv()
            forward_copy(k).start()
            field[1:rows + 1, place(k), lanes(0)] = cell_block(arecv[0, k])
        for side in (0, 1):
            @pl.when(gets[side])
            def _():
                for k in order:
                    halo_copy(side, k).wait_recv()
                halo_forward(side).start()
        for k in [0] + away:
            forward_copy(k).wait_recv()
            field[1:rows + 1, place(k), lanes(1)] = cell_block(arecv[1, k])
        for side in (0, 1):
            @pl.when(gets[side])
            def _():
                halo_forward(side).wait_recv()
                for p in (0, 1):
                    for k in order:
                        field[(0, rows + 1)[side], place(k), lanes(p)] = hrecv[side, p, k].astype(f32)[:cols]

            @pl.when(jnp.logical_not(gets[side]))
            def _():
                fold(side)
        spread()

    def assemble_two(act):
        bpack[...] = act.astype(bf16)
        band_copy().start()
        band = unpack(act, all_cells)
        epack[0] = band[all_cells - all_cols:].astype(bf16)
        epack[1] = band[:all_cols].astype(bf16)
        for side in (0, 1):
            @pl.when(sends[side])
            def _():
                for p in (1, 0):
                    edge_copy(side, p).start()
        field[1:rows + 1, inside, lanes(0)] = band.reshape(rows, all_cols, part)
        band_copy().wait_recv()
        other = unpack(brecv[...].astype(f32), all_cells)
        field[1:rows + 1, inside, lanes(1)] = other.reshape(rows, all_cols, part)
        for side in (0, 1):
            @pl.when(gets[side])
            def _():
                for p in (0, 1):
                    edge_copy(side, p).wait_recv()
                    field[(0, rows + 1)[side], inside, lanes(p)] = erecv[side, p].astype(f32)

            @pl.when(jnp.logical_not(gets[side]))
            def _():
                fold(side)
        spread()

    def multiply(conv, slot):
        local, other = weights[conv, slot]
        local.wait()
        other.wait_recv()
        total = None
        for a in range(3):
            term = jnp.dot(
                taps[a:a + rows].reshape(all_cells, 6 * part),
                w[conv, slot, a].reshape(6 * part, width),
                preferred_element_type=f32,
            )
            total = term if total is None else total + term
        return total

    features = x_ref[0].astype(f32).reshape(cells, width)
    act = silu(features)
    fill = jnp.zeros((hpack.shape[2] - cols, part), f32)
    for j in range(n_lon):
        piece = act[:, lanes(j)]
        apack[j] = pack(piece, half).astype(bf16)
        hpack[0, j] = jnp.concatenate([piece[cells - cols:], fill], axis=0).astype(bf16)
        hpack[1, j] = jnp.concatenate([piece[:cols], fill], axis=0).astype(bf16)
    pl.semaphore_wait(barrier, greeted)
    for slot in (1, 0):
        weights[0, slot][1].start()
    exchange_one()
    assemble_one()

    total = multiply(0, 1)
    for j in range(n_lon):
        ysend1[j] = pack(total[:, lanes(j)], band_half).astype(bf16)
    for k in order:
        far_copy(0, k).start()
    total = multiply(0, 0)
    for j in range(n_lon):
        own[j] = pack(total[:, lanes(j)], band_half)
    for slot in (1, 0):
        weights[1, slot][1].start()
    hidden = None
    for k in order:
        far_copy(0, k).wait_recv()
        slot = (lon + k) % n_lon
        value = own[slot] + yrecv1[slot].astype(f32)
        if k:
            zsend1[k] = value.astype(bf16)
            along_copy(0, k).start()
        else:
            hidden = value
    for k in away:
        along_copy(0, k).wait_recv()
        hidden = hidden + zrecv1[k].astype(f32)
    bias = b1_ref[:, lanes(0)]
    for j in away:
        bias = jnp.where(lon == j, b1_ref[:, lanes(j)], bias)
    assemble_two(silu(hidden + jnp.concatenate([bias, bias], axis=1)))

    def chunk(slot, k):
        start = pl.multiple_of(((lon + k) % n_lon) * cols, 8)
        return acc[slot, :, pl.ds(start, cols), :].reshape(cells, width)

    def padded(value):
        spare = jnp.zeros((ysend2.shape[1] - cells, width), f32)
        return jnp.concatenate([value, spare], axis=0).astype(bf16)

    acc[1] = multiply(1, 1).reshape(rows, all_cols, width)
    for k in order:
        ysend2[(lon + k) % n_lon] = padded(chunk(1, k))
        far_copy(1, k).start()
    acc[0] = multiply(1, 0).reshape(rows, all_cols, width)
    second = None
    for k in order:
        far_copy(1, k).wait_recv()
        value = chunk(0, k) + yrecv2[(lon + k) % n_lon].astype(f32)[:cells]
        if k:
            zsend2[k] = padded(value)
            along_copy(1, k).start()
        else:
            second = value
    for k in away:
        along_copy(1, k).wait_recv()
        second = second + zrecv2[k].astype(f32)[:cells]
    out_ref[0] = (second + b2_ref[...]).reshape(rows, cols, width)

    for k in order:
        forward_copy(k).wait_send()
        if k:
            main_copy(k).wait_send()
    band_copy().wait_send()
    for side in (0, 1):
        @pl.when(sends[side])
        def _():
            for k in order:
                halo_copy(side, k).wait_send()
            for p in (0, 1):
                edge_copy(side, p).wait_send()

        @pl.when(gets[side])
        def _():
            halo_forward(side).wait_send()
    for conv in (0, 1):
        for slot in (0, 1):
            weights[conv, slot][1].wait_send()
        for k in order:
            far_copy(conv, k).wait_send()
            if k:
                along_copy(conv, k).wait_send()


def body(n_lat, n_lon, features, kernel_one, bias_one, kernel_two, bias_two):
    _, rows, cols, width = features.shape
    cells, part, all_cols = rows * cols, width // n_lon, cols * n_lon
    half = round_up(-(-cells // 2), 16)
    band_half = round_up(-(-rows * all_cols // 2), 16)
    tall, short = round_up(cells, 16), round_up(cols, 16)
    bf16, f32 = jnp.bfloat16, jnp.float32
    dma = pltpu.SemaphoreType.DMA
    vmem = pl.BlockSpec(memory_space=pltpu.VMEM)
    anywhere = pl.BlockSpec(memory_space=pl.ANY)
    second = pl.pallas_call(
        functools.partial(block_kernel, n_lat, n_lon),
        out_shape=jax.ShapeDtypeStruct(features.shape, f32),
        in_specs=[vmem, anywhere, vmem, anywhere, vmem],
        out_specs=vmem,
        scratch_shapes=[
            pltpu.VMEM((2, 2, 3, 3, 2, part, width), bf16),
            pltpu.VMEM((n_lon, half, 2 * part), bf16),
            pltpu.VMEM((2, n_lon, half, 2 * part), bf16),
            pltpu.VMEM((2, n_lon, short, part), bf16),
            pltpu.VMEM((2, 2, n_lon, short, part), bf16),
            pltpu.VMEM((band_half, 2 * part), bf16),
            pltpu.VMEM((band_half, 2 * part), bf16),
            pltpu.VMEM((2, all_cols, part), bf16),
            pltpu.VMEM((2, 2, all_cols, part), bf16),
            pltpu.VMEM((rows + 2, all_cols + 2 * EDGE, 2 * part), f32),
            pltpu.VMEM((rows + 2, all_cols, 6 * part), bf16),
            pltpu.VMEM((n_lon, band_half, 2 * part), f32),
            pltpu.VMEM((n_lon, band_half, 2 * part), bf16),
            pltpu.VMEM((n_lon, band_half, 2 * part), bf16),
            pltpu.VMEM((n_lon, band_half, 2 * part), bf16),
            pltpu.VMEM((n_lon, band_half, 2 * part), bf16),
            pltpu.VMEM((2, rows, all_cols, width), f32),
            pltpu.VMEM((n_lon, tall, width), bf16),
            pltpu.VMEM((n_lon, tall, width), bf16),
            pltpu.VMEM((n_lon, tall, width), bf16),
            pltpu.VMEM((n_lon, tall, width), bf16),
            dma((2, 2)), dma((2, 2)), dma((2, 2)),
            dma((2, n_lon)), dma((2, n_lon)),
            dma((2, n_lon)), dma((2, n_lon)), dma((2,)), dma((2,)),
            dma, dma, dma((2, 2)), dma((2, 2)),
            dma((2, n_lon)), dma((2, n_lon)), dma((2, n_lon)), dma((2, n_lon)),
        ],
        compiler_params=pltpu.CompilerParams(
            collective_id=0, has_side_effects=True, vmem_limit_bytes=56 * 2**20
        ),
        name="residual_block",
    )(features, kernel_one, bias_one.reshape(1, width), kernel_two, bias_two.reshape(1, width))
    return ((features.astype(f32) + second) * skip_scale).astype(bf16)


def solution(mesh):
    placed = (
        P(None, "lat", "lon", "ch"),
        P(None, None, "ch", "lon", None),
        P("ch"),
        P(None, None, "ch", "lon", None),
        P("ch"),
    )
    return jax.shard_map(
        functools.partial(body, mesh.shape["lat"], mesh.shape["lon"]),
        mesh=mesh, in_specs=placed, out_specs=P(None, "lat", "lon", "ch"), check_vma=False,
    )
```

time: 55.8 us -> 48.1 us (0.86)
  Pallas kernels: 54.1 us -> 46.3 us
  other arithmetic: 0 us -> 1.58 us
  local copies, waits for them, and re-layouts: 1.53 us -> 0.01 us
    pallas_call x1, Pallas kernels: 54.1 us -> 46.3 us  [body(): pl.pallas_call(functools.partial(block_kernel, n_lat, n_lon), out_shape=j...]
    convert_element_type x0 -> x1, other arithmetic: none -> 1.58 us  [body(): return ((features.astype(f32) + second) * skip_scale).astype(bf16)]
    unnamed x1 -> x2, local copies, waits for them, and re-layouts: 1.53 us -> 0.01 us
where the time goes in v3:
time: 48.1 us; the launch traced here: 47.9 us
  Pallas kernels  46.3 us (96%)
  other arithmetic  1.58 us (3%)
    pallas_call x1, Pallas kernels, body(): pl.pallas_call(functools.partial(block_kernel, n_lat, n_lon), out_shape=j...  46.3 us
    convert_element_type x1, other arithmetic, body(): return ((features.astype(f32) + second) * skip_scale).astype(bf16)  1.58 us

profile of v3, /device:TPU:0, one launch (start us, length us, event | category | flops | bytes accessed | tf_op | source)
XLA Modules:
  0.0 47.9 jit_solution(4215640526788249536)
XLA Ops:
  0.0 0.0 copy-start
  0.0 46.3 %residual_block.1 = f32[1,7,24,256]{3,2,1,0:T(8,128)} custom-call(bf16[1,7,24,256]{3,2,1,0:T(8,128)(2,1)} %x_ref.1, bf16[3,3,1,64,1024]{4,3,2,1,0:T(8,128)(2,1)} %k1_ref.1, f32[1,256]{1,0:T(1,128)} %bitcast.2, bf16[3,3,1,64,1024]{4,3,2,1,0:T(8,128)(2,1)} %k2_ref.1, f32[1,256]{1,0:T(1,128)} %bitcast.3), custom_call_target="tpu_custom_call" | custom-call | tf_op jit(solution)/shard_map/residual_block/pallas_call | solution.py:346
  46.3 0.0 copy-done
  46.3 1.6 %multiply_convert_fusion = bf16[1,7,24,256]{3,2,1,0:T(8,128)(2,1)} fusion(f32[1,7,24,256]{3,2,1,0:T(8,128)} %residual_block.1, bf16[1,7,24,256]{3,2,1,0:T(8,128)(2,1)S(1)} %copy-done), kind=kLoop, calls=%fused_computation | loop fusion | flops 172032 | bytes 344064 | tf_op jit(solution)/shard_map/convert_element_type | solution.py:384
Async XLA Ops:
  0.0 46.3 %copy-start = (bf16[1,7,24,256]{3,2,1,0:T(8,128)(2,1)S(1)}, bf16[1,7,24,256]{3,2,1,0:T(8,128)(2,1)}, u32[]{:S(2)}) copy-start(bf16[1,7,24,256]{3,2,1,0:T(8,128)(2,1)} %x_ref.1) | copy-start | bytes 258052

commit v4 on v3

--- a/solution.py
+++ b/solution.py
@@ -33,10 +33,19 @@
     return jnp.concatenate([block[:, :part], block[:count - half, part:]], axis=0)
 
 
+def row_groups(rows, per_row, packed):
+    groups, offset, first = [], 0, 0
+    for count in (-(-rows // 2), rows // 2):
+        size = round_up(-(-count * per_row // packed), 16)
+        groups.append((first, count, offset, size))
+        first, offset = first + count, offset + size
+    return groups, offset
+
+
 def block_kernel(
     n_lat, n_lon, x_ref, k1_ref, b1_ref, k2_ref, b2_ref, out_ref,
     w, apack, arecv, hpack, hrecv, bpack, brecv, epack, erecv, field, taps,
-    own, ysend1, yrecv1, zsend1, zrecv1, acc, ysend2, yrecv2, zsend2, zrecv2,
+    own, kept, ysend1, yrecv1, zsend1, zrecv1, acc, ysend2, yrecv2, zsend2, zrecv2,
     wl_sem, ws_sem, wr_sem, as_sem, ar_sem, hs_sem, hr_sem, fs_sem, fr_sem,
     bs_sem, br_sem, es_sem, er_sem, ys_sem, yr_sem, zs_sem, zr_sem,
 ):
@@ -45,8 +54,8 @@
     part = width // n_lon
     half = apack.shape[1]
     all_cols = cols * n_lon
-    all_cells = rows * all_cols
-    band_half = bpack.shape[0]
+    bands = row_groups(rows, all_cols, 2)[0]
+    blocks = row_groups(rows, cols, 1)[0]
     f32, bf16 = jnp.float32, jnp.bfloat16
     lat, lon, ch = lax.axis_index("lat"), lax.axis_index("lon"), lax.axis_index("ch")
     near = ch + 1 - 2 * (ch % 2)
@@ -117,8 +126,9 @@
             hrecv.at[side, 0], hrecv.at[side, 1], fs_sem.at[side], fr_sem.at[side], device(0, 0, near)
         )
 
-    def band_copy():
-        return remote(bpack, brecv, bs_sem, br_sem, device(0, 0, near))
+    def band_copy(g):
+        place = pl.ds(bands[g][2], bands[g][3])
+        return remote(bpack.at[place], brecv.at[place], bs_sem.at[g], br_sem.at[g], device(0, 0, near))
 
     def edge_copy(side, p):
         return remote(
@@ -126,14 +136,24 @@
             device((1, -1)[side] % n_lat, 0, (ch, near)[p]),
         )
 
-    def far_copy(conv, k):
+    def piece_of(conv, g):
+        return pl.ds(*(bands, blocks)[conv][g][2:])
+
+    def far_copy(conv, g, k):
         src, dst = ((ysend1, yrecv1), (ysend2, yrecv2))[conv]
-        slot = (lon + k) % n_lon
-        return remote(src.at[slot], dst.at[slot], ys_sem.at[conv, k], yr_sem.at[conv, k], device(0, 0, far))
-
-    def along_copy(conv, k):
+        slot, piece = (lon + k) % n_lon, piece_of(conv, g)
+        return remote(
+            src.at[slot, piece], dst.at[slot, piece],
+            ys_sem.at[conv, g, k], yr_sem.at[conv, g, k], device(0, 0, far),
+        )
+
+    def along_copy(conv, g, k):
         src, dst = ((zsend1, zrecv1), (zsend2, zrecv2))[conv]
-        return remote(src.at[k], dst.at[k], zs_sem.at[conv, k], zr_sem.at[conv, k], device(0, k, ch))
+        piece = piece_of(conv, g)
+        return remote(
+            src.at[k, piece], dst.at[k, piece],
+            zs_sem.at[conv, g, k], zr_sem.at[conv, g, k], device(0, k, ch),
+        )
 
     def lanes(p):
         return slice(p * part, (p + 1) * part)
@@ -198,21 +218,26 @@
                 fold(side)
         spread()
 
-    def assemble_two(act):
-        bpack[...] = act.astype(bf16)
-        band_copy().start()
-        band = unpack(act, all_cells)
-        epack[0] = band[all_cells - all_cols:].astype(bf16)
-        epack[1] = band[:all_cols].astype(bf16)
+    def hand_on(g, act):
+        first, count, offset, size = bands[g]
+        bpack[offset:offset + size] = act.astype(bf16)
+        band_copy(g).start()
+        band = unpack(act, count * all_cols)
         for side in (0, 1):
-            @pl.when(sends[side])
-            def _():
-                for p in (1, 0):
-                    edge_copy(side, p).start()
-        field[1:rows + 1, inside, lanes(0)] = band.reshape(rows, all_cols, part)
-        band_copy().wait_recv()
-        other = unpack(brecv[...].astype(f32), all_cells)
-        field[1:rows + 1, inside, lanes(1)] = other.reshape(rows, all_cols, part)
+            if g == (1, 0)[side]:
+                epack[side] = (band[-all_cols:], band[:all_cols])[side].astype(bf16)
+
+                @pl.when(sends[side])
+                def _():
+                    for p in (1, 0):
+                        edge_copy(side, p).start()
+        field[first + 1:first + 1 + count, inside, lanes(0)] = band.reshape(count, all_cols, part)
+
+    def assemble_two():
+        for g, (first, count, offset, size) in enumerate(bands):
+            band_copy(g).wait_recv()
+            other = unpack(brecv[offset:offset + size].astype(f32), count * all_cols)
+            field[first + 1:first + 1 + count, inside, lanes(1)] = other.reshape(count, all_cols, part)
         for side in (0, 1):
             @pl.when(gets[side])
             def _():
@@ -225,14 +250,17 @@
                 fold(side)
         spread()
 
-    def multiply(conv, slot):
+    def weights_here(conv, slot):
         local, other = weights[conv, slot]
         local.wait()
         other.wait_recv()
+
+    def multiply(conv, slot, g):
+        first, count = bands[g][:2]
         total = None
         for a in range(3):
             term = jnp.dot(
-                taps[a:a + rows].reshape(all_cells, 6 * part),
+                taps[first + a:first + a + count].reshape(count * all_cols, 6 * part),
                 w[conv, slot, a].reshape(6 * part, width),
                 preferred_element_type=f32,
             )
@@ -253,66 +281,83 @@
     exchange_one()
     assemble_one()
 
-    total = multiply(0, 1)
-    for j in range(n_lon):
-        ysend1[j] = pack(total[:, lanes(j)], band_half).astype(bf16)
-    for k in order:
-        far_copy(0, k).start()
-    total = multiply(0, 0)
-    for j in range(n_lon):
-        own[j] = pack(total[:, lanes(j)], band_half)
+    weights_here(0, 1)
+    for g, (_, _, offset, size) in enumerate(bands):
+        total = multiply(0, 1, g)
+        for j in range(n_lon):
+            ysend1[j, offset:offset + size] = pack(total[:, lanes(j)], size).astype(bf16)
+        for k in order:
+            far_copy(0, g, k).start()
+    weights_here(0, 0)
+    for g, (_, _, offset, size) in enumerate(bands):
+        total = multiply(0, 0, g)
+        for j in range(n_lon):
+            own[j, offset:offset + size] = pack(total[:, lanes(j)], size)
     for slot in (1, 0):
         weights[1, slot][1].start()
-    hidden = None
-    for k in order:
-        far_copy(0, k).wait_recv()
-        slot = (lon + k) % n_lon
-        value = own[slot] + yrecv1[slot].astype(f32)
-        if k:
-            zsend1[k] = value.astype(bf16)
-            along_copy(0, k).start()
-        else:
-            hidden = value
-    for k in away:
-        along_copy(0, k).wait_recv()
-        hidden = hidden + zrecv1[k].astype(f32)
+    for g, (_, _, offset, size) in enumerate(bands):
+        for k in order:
+            far_copy(0, g, k).wait_recv()
+            slot = (lon + k) % n_lon
+            value = own[slot, offset:offset + size] + yrecv1[slot, offset:offset + size].astype(f32)
+            if k:
+                zsend1[k, offset:offset + size] = value.astype(bf16)
+                along_copy(0, g, k).start()
+            else:
+                kept[offset:offset + size] = value
     bias = b1_ref[:, lanes(0)]
     for j in away:
         bias = jnp.where(lon == j, b1_ref[:, lanes(j)], bias)
-    assemble_two(silu(hidden + jnp.concatenate([bias, bias], axis=1)))
-
-    def chunk(slot, k):
+    bias = jnp.concatenate([bias, bias], axis=1)
+    for g, (_, _, offset, size) in enumerate(bands):
+        hidden = kept[offset:offset + size]
+        for k in away:
+            along_copy(0, g, k).wait_recv()
+            hidden = hidden + zrecv1[k, offset:offset + size].astype(f32)
+        hand_on(g, silu(hidden + bias))
+    assemble_two()
+
+    def chunk(slot, g, k):
+        first, count = blocks[g][:2]
         start = pl.multiple_of(((lon + k) % n_lon) * cols, 8)
-        return acc[slot, :, pl.ds(start, cols), :].reshape(cells, width)
-
-    def padded(value):
-        spare = jnp.zeros((ysend2.shape[1] - cells, width), f32)
-        return jnp.concatenate([value, spare], axis=0).astype(bf16)
-
-    acc[1] = multiply(1, 1).reshape(rows, all_cols, width)
-    for k in order:
-        ysend2[(lon + k) % n_lon] = padded(chunk(1, k))
-        far_copy(1, k).start()
-    acc[0] = multiply(1, 0).reshape(rows, all_cols, width)
-    second = None
-    for k in order:
-        far_copy(1, k).wait_recv()
-        value = chunk(0, k) + yrecv2[(lon + k) % n_lon].astype(f32)[:cells]
-        if k:
-            zsend2[k] = padded(value)
-            along_copy(1, k).start()
-        else:
-            second = value
-    for k in away:
-        along_copy(1, k).wait_recv()
-        second = second + zrecv2[k].astype(f32)[:cells]
-    out_ref[0] = (second + b2_ref[...]).reshape(rows, cols, width)
+        return acc[slot, first:first + count, pl.ds(start, cols), :].reshape(count * cols, width)
+
+    def padded(value, size):
+        if size > value.shape[0]:
+            value = jnp.concatenate([value, jnp.zeros((size - value.shape[0], width), f32)], axis=0)
+        return value.astype(bf16)
+
+    for slot in (1, 0):
+        weights_here(1, slot)
+        for g, (first, count, offset, size) in enumerate(blocks):
+            acc[slot, first:first + count] = multiply(1, slot, g).reshape(count, all_cols, width)
+            if slot:
+                for k in order:
+                    ysend2[(lon + k) % n_lon, offset:offset + size] = padded(chunk(1, g, k), size)
+                    far_copy(1, g, k).start()
+    for g, (first, count, offset, size) in enumerate(blocks):
+        for k in order:
+            far_copy(1, g, k).wait_recv()
+            other = yrecv2[(lon + k) % n_lon, offset:offset + size].astype(f32)
+            value = chunk(0, g, k) + other[:count * cols]
+            if k:
+                zsend2[k, offset:offset + size] = padded(value, size)
+                along_copy(1, g, k).start()
+            else:
+                out_ref[0, first:first + count] = (value + b2_ref[...]).reshape(count, cols, width)
+    for g, (first, count, offset, size) in enumerate(blocks):
+        second = out_ref[0, first:first + count].reshape(count * cols, width)
+        for k in away:
+            along_copy(1, g, k).wait_recv()
+            second = second + zrecv2[k, offset:offset + size].astype(f32)[:count * cols]
+        out_ref[0, first:first + count] = second.reshape(count, cols, width)
 
     for k in order:
         forward_copy(k).wait_send()
         if k:
             main_copy(k).wait_send()
-    band_copy().wait_send()
+    for g in (0, 1):
+        band_copy(g).wait_send()
     for side in (0, 1):
         @pl.when(sends[side])
         def _():
@@ -327,18 +372,19 @@
     for conv in (0, 1):
         for slot in (0, 1):
             weights[conv, slot][1].wait_send()
-        for k in order:
-            far_copy(conv, k).wait_send()
-            if k:
-                along_copy(conv, k).wait_send()
+        for g in (0, 1):
+            for k in order:
+                far_copy(conv, g, k).wait_send()
+                if k:
+                    along_copy(conv, g, k).wait_send()
 
 
 def body(n_lat, n_lon, features, kernel_one, bias_one, kernel_two, bias_two):
     _, rows, cols, width = features.shape
     cells, part, all_cols = rows * cols, width // n_lon, cols * n_lon
     half = round_up(-(-cells // 2), 16)
-    band_half = round_up(-(-rows * all_cols // 2), 16)
-    tall, short = round_up(cells, 16), round_up(cols, 16)
+    band_half, tall = row_groups(rows, all_cols, 2)[1], row_groups(rows, cols, 1)[1]
+    short = round_up(cols, 16)
     bf16, f32 = jnp.bfloat16, jnp.float32
     dma = pltpu.SemaphoreType.DMA
     vmem = pl.BlockSpec(memory_space=pltpu.VMEM)
@@ -361,6 +407,7 @@
             pltpu.VMEM((rows + 2, all_cols + 2 * EDGE, 2 * part), f32),
             pltpu.VMEM((rows + 2, all_cols, 6 * part), bf16),
             pltpu.VMEM((n_lon, band_half, 2 * part), f32),
+            pltpu.VMEM((band_half, 2 * part), f32),
             pltpu.VMEM((n_lon, band_half, 2 * part), bf16),
             pltpu.VMEM((n_lon, band_half, 2 * part), bf16),
             pltpu.VMEM((n_lon, band_half, 2 * part), bf16),
@@ -373,8 +420,8 @@
             dma((2, 2)), dma((2, 2)), dma((2, 2)),
             dma((2, n_lon)), dma((2, n_lon)),
             dma((2, n_lon)), dma((2, n_lon)), dma((2,)), dma((2,)),
-            dma, dma, dma((2, 2)), dma((2, 2)),
-            dma((2, n_lon)), dma((2, n_lon)), dma((2, n_lon)), dma((2, n_lon)),
+            dma((2,)), dma((2,)), dma((2, 2)), dma((2, 2)),
+            dma((2, 2, n_lon)), dma((2, 2, n_lon)), dma((2, 2, n_lon)), dma((2, 2, n_lon)),
         ],
         compiler_params=pltpu.CompilerParams(
             collective_id=0, has_side_effects=True, vmem_limit_bytes=56 * 2**20

time: 48.1 us -> 44.8 us (0.931)
  Pallas kernels: 46.3 us -> 43 us
    pallas_call x1, Pallas kernels: 46.3 us -> 43 us  [body(): pl.pallas_call(functools.partial(block_kernel, n_lat, n_lon), out_shape=j...]
where the time goes in v4:
time: 44.8 us; the launch traced here: 44.6 us
  Pallas kernels  43 us (96%)
  other arithmetic  1.58 us (4%)
    pallas_call x1, Pallas kernels, body(): pl.pallas_call(functools.partial(block_kernel, n_lat, n_lon), out_shape=j...  43 us
    convert_element_type x1, other arithmetic, body(): return ((features.astype(f32) + second) * skip_scale).astype(bf16)  1.58 us

profile of v4, /device:TPU:0, one launch (start us, length us, event | category | flops | bytes accessed | tf_op | source)
XLA Modules:
  0.0 44.6 jit_solution(4876881111573545255)
XLA Ops:
  0.0 0.0 copy-start
  0.0 43.0 %residual_block.1 = f32[1,7,24,256]{3,2,1,0:T(8,128)} custom-call(bf16[1,7,24,256]{3,2,1,0:T(8,128)(2,1)} %x_ref.1, bf16[3,3,1,64,1024]{4,3,2,1,0:T(8,128)(2,1)} %k1_ref.1, f32[1,256]{1,0:T(1,128)} %bitcast.2, bf16[3,3,1,64,1024]{4,3,2,1,0:T(8,128)(2,1)} %k2_ref.1, f32[1,256]{1,0:T(1,128)} %bitcast.3), custom_call_target="tpu_custom_call" | custom-call | tf_op jit(solution)/shard_map/residual_block/pallas_call | solution.py:392
  43.0 0.0 copy-done
  43.0 1.6 %multiply_convert_fusion = bf16[1,7,24,256]{3,2,1,0:T(8,128)(2,1)} fusion(f32[1,7,24,256]{3,2,1,0:T(8,128)} %residual_block.1, bf16[1,7,24,256]{3,2,1,0:T(8,128)(2,1)S(1)} %copy-done), kind=kLoop, calls=%fused_computation | loop fusion | flops 172032 | bytes 344064 | tf_op jit(solution)/shard_map/convert_element_type | solution.py:431
Async XLA Ops:
  0.0 43.0 %copy-start = (bf16[1,7,24,256]{3,2,1,0:T(8,128)(2,1)S(1)}, bf16[1,7,24,256]{3,2,1,0:T(8,128)(2,1)}, u32[]{:S(2)}) copy-start(bf16[1,7,24,256]{3,2,1,0:T(8,128)(2,1)} %x_ref.1) | copy-start | bytes 258052

commit v5 on v4

--- a/solution.py
+++ b/solution.py
@@ -33,13 +33,18 @@
     return jnp.concatenate([block[:, :part], block[:count - half, part:]], axis=0)
 
 
-def row_groups(rows, per_row, packed):
-    groups, offset, first = [], 0, 0
-    for count in (-(-rows // 2), rows // 2):
+def row_groups(counts, per_row, packed):
+    groups, offset = [], 0
+    for count in counts:
         size = round_up(-(-count * per_row // packed), 16)
-        groups.append((first, count, offset, size))
-        first, offset = first + count, offset + size
+        groups.append((count, offset, size))
+        offset += size
     return groups, offset
+
+
+def row_counts(rows):
+    ahead = -(-rows // 2)
+    return (ahead, rows - ahead), (ahead - 1, rows - ahead + 1)
 
 
 def block_kernel(
@@ -54,10 +59,12 @@
     part = width // n_lon
     half = apack.shape[1]
     all_cols = cols * n_lon
-    bands = row_groups(rows, all_cols, 2)[0]
-    blocks = row_groups(rows, cols, 1)[0]
+    counts = row_counts(rows)
+    bands = row_groups(counts[0], all_cols, 2)[0]
+    blocks = row_groups(counts[1], cols, 1)[0]
     f32, bf16 = jnp.float32, jnp.bfloat16
     lat, lon, ch = lax.axis_index("lat"), lax.axis_index("lon"), lax.axis_index("ch")
+    flip = lat >= n_lat - n_lat // 2
     near = ch + 1 - 2 * (ch % 2)
     far = ch + 2 - 4 * ((ch // 2) % 2)
     near_far = near + 2 - 4 * ((near // 2) % 2)
@@ -127,7 +134,7 @@
         )
 
     def band_copy(g):
-        place = pl.ds(bands[g][2], bands[g][3])
+        place = pl.ds(*bands[g][1:])
         return remote(bpack.at[place], brecv.at[place], bs_sem.at[g], br_sem.at[g], device(0, 0, near))
 
     def edge_copy(side, p):
@@ -137,7 +144,7 @@
         )
 
     def piece_of(conv, g):
-        return pl.ds(*(bands, blocks)[conv][g][2:])
+        return pl.ds(*(bands, blocks)[conv][g][1:])
 
     def far_copy(conv, g, k):
         src, dst = ((ysend1, yrecv1), (ysend2, yrecv2))[conv]
@@ -154,6 +161,10 @@
             src.at[k, piece], dst.at[k, piece],
             zs_sem.at[conv, g, k], zr_sem.at[conv, g, k], device(0, k, ch),
         )
+
+    def first_row(conv, g):
+        ahead, behind = counts[conv]
+        return jnp.where(flip, (behind, 0)[g], (0, ahead)[g])
 
     def lanes(p):
         return slice(p * part, (p + 1) * part)
@@ -166,12 +177,13 @@
         field[row, EDGE:EDGE + turn] = field[inner, EDGE + turn:EDGE + all_cols]
         field[row, EDGE + turn:EDGE + all_cols] = field[inner, EDGE:EDGE + turn]
 
-    def spread():
-        field[:, EDGE - 1:EDGE] = field[:, EDGE + all_cols - 1:EDGE + all_cols]
-        field[:, EDGE + all_cols:EDGE + all_cols + 1] = field[:, EDGE:EDGE + 1]
+    def spread(first, count):
+        here = pl.ds(first, count)
+        field[here, EDGE - 1:EDGE] = field[here, EDGE + all_cols - 1:EDGE + all_cols]
+        field[here, EDGE + all_cols:EDGE + all_cols + 1] = field[here, EDGE:EDGE + 1]
         for e in range(3):
-            taps[:, :, e * 2 * part:(e + 1) * 2 * part] = field[
-                :, EDGE - 1 + e:EDGE - 1 + e + all_cols
+            taps[here, :, e * 2 * part:(e + 1) * 2 * part] = field[
+                here, EDGE - 1 + e:EDGE - 1 + e + all_cols
             ].astype(bf16)
 
     def exchange_one():
@@ -216,39 +228,42 @@
             @pl.when(jnp.logical_not(gets[side]))
             def _():
                 fold(side)
-        spread()
+        spread(0, rows + 2)
 
     def hand_on(g, act):
-        first, count, offset, size = bands[g]
+        count, offset, size = bands[g]
         bpack[offset:offset + size] = act.astype(bf16)
         band_copy(g).start()
         band = unpack(act, count * all_cols)
         for side in (0, 1):
-            if g == (1, 0)[side]:
+            turned = flip if side == g else jnp.logical_not(flip)
+
+            @pl.when(jnp.logical_and(sends[side], turned))
+            def _():
                 epack[side] = (band[-all_cols:], band[:all_cols])[side].astype(bf16)
-
-                @pl.when(sends[side])
-                def _():
-                    for p in (1, 0):
-                        edge_copy(side, p).start()
-        field[first + 1:first + 1 + count, inside, lanes(0)] = band.reshape(count, all_cols, part)
-
-    def assemble_two():
-        for g, (first, count, offset, size) in enumerate(bands):
-            band_copy(g).wait_recv()
-            other = unpack(brecv[offset:offset + size].astype(f32), count * all_cols)
-            field[first + 1:first + 1 + count, inside, lanes(1)] = other.reshape(count, all_cols, part)
+                for p in (1, 0):
+                    edge_copy(side, p).start()
+        field[pl.ds(first_row(0, g) + 1, count), inside, lanes(0)] = band.reshape(count, all_cols, part)
+
+    def assemble_two(g):
+        count, offset, size = bands[g]
+        band_copy(g).wait_recv()
+        other = unpack(brecv[offset:offset + size].astype(f32), count * all_cols)
+        field[pl.ds(first_row(0, g) + 1, count), inside, lanes(1)] = other.reshape(count, all_cols, part)
         for side in (0, 1):
-            @pl.when(gets[side])
+            due = jnp.logical_not(flip) if side == g else flip
+
+            @pl.when(jnp.logical_and(gets[side], due))
             def _():
                 for p in (0, 1):
                     edge_copy(side, p).wait_recv()
                     field[(0, rows + 1)[side], inside, lanes(p)] = erecv[side, p].astype(f32)
 
-            @pl.when(jnp.logical_not(gets[side]))
+            @pl.when(jnp.logical_and(jnp.logical_not(gets[side]), due))
             def _():
                 fold(side)
-        spread()
+        count += 1
+        spread(jnp.where(flip, (rows + 2 - count, 0)[g], (0, rows + 2 - count)[g]), count)
 
     def weights_here(conv, slot):
         local, other = weights[conv, slot]
@@ -256,11 +271,11 @@
         other.wait_recv()
 
     def multiply(conv, slot, g):
-        first, count = bands[g][:2]
+        first, count = first_row(conv, g), counts[conv][g]
         total = None
         for a in range(3):
             term = jnp.dot(
-                taps[first + a:first + a + count].reshape(count * all_cols, 6 * part),
+                taps[pl.ds(first + a, count)].reshape(count * all_cols, 6 * part),
                 w[conv, slot, a].reshape(6 * part, width),
                 preferred_element_type=f32,
             )
@@ -282,20 +297,20 @@
     assemble_one()
 
     weights_here(0, 1)
-    for g, (_, _, offset, size) in enumerate(bands):
+    for g, (_, offset, size) in enumerate(bands):
         total = multiply(0, 1, g)
         for j in range(n_lon):
             ysend1[j, offset:offset + size] = pack(total[:, lanes(j)], size).astype(bf16)
         for k in order:
             far_copy(0, g, k).start()
     weights_here(0, 0)
-    for g, (_, _, offset, size) in enumerate(bands):
+    for g, (_, offset, size) in enumerate(bands):
         total = multiply(0, 0, g)
         for j in range(n_lon):
             own[j, offset:offset + size] = pack(total[:, lanes(j)], size)
     for slot in (1, 0):
         weights[1, slot][1].start()
-    for g, (_, _, offset, size) in enumerate(bands):
+    for g, (_, offset, size) in enumerate(bands):
         for k in order:
             far_copy(0, g, k).wait_recv()
             slot = (lon + k) % n_lon
@@ -309,33 +324,35 @@
     for j in away:
         bias = jnp.where(lon == j, b1_ref[:, lanes(j)], bias)
     bias = jnp.concatenate([bias, bias], axis=1)
-    for g, (_, _, offset, size) in enumerate(bands):
+
+    def chunk(slot, g, k):
+        count = counts[1][g]
+        start = pl.multiple_of(((lon + k) % n_lon) * cols, 8)
+        return acc[slot, pl.ds(first_row(1, g), count), pl.ds(start, cols), :].reshape(count * cols, width)
+
+    def padded(value, size):
+        if size > value.shape[0]:
+            value = jnp.concatenate([value, jnp.zeros((size - value.shape[0], width), f32)], axis=0)
+        return value.astype(bf16)
+
+    def multiply_two(slot, g):
+        count, offset, size = blocks[g]
+        acc[slot, pl.ds(first_row(1, g), count)] = multiply(1, slot, g).reshape(count, all_cols, width)
+        if slot:
+            for k in order:
+                ysend2[(lon + k) % n_lon, offset:offset + size] = padded(chunk(1, g, k), size)
+                far_copy(1, g, k).start()
+
+    def gather_one(g):
+        _, offset, size = bands[g]
         hidden = kept[offset:offset + size]
         for k in away:
             along_copy(0, g, k).wait_recv()
             hidden = hidden + zrecv1[k, offset:offset + size].astype(f32)
         hand_on(g, silu(hidden + bias))
-    assemble_two()
-
-    def chunk(slot, g, k):
-        first, count = blocks[g][:2]
-        start = pl.multiple_of(((lon + k) % n_lon) * cols, 8)
-        return acc[slot, first:first + count, pl.ds(start, cols), :].reshape(count * cols, width)
-
-    def padded(value, size):
-        if size > value.shape[0]:
-            value = jnp.concatenate([value, jnp.zeros((size - value.shape[0], width), f32)], axis=0)
-        return value.astype(bf16)
-
-    for slot in (1, 0):
-        weights_here(1, slot)
-        for g, (first, count, offset, size) in enumerate(blocks):
-            acc[slot, first:first + count] = multiply(1, slot, g).reshape(count, all_cols, width)
-            if slot:
-                for k in order:
-                    ysend2[(lon + k) % n_lon, offset:offset + size] = padded(chunk(1, g, k), size)
-                    far_copy(1, g, k).start()
-    for g, (first, count, offset, size) in enumerate(blocks):
+
+    def scatter_two(g):
+        count, offset, size = blocks[g]
         for k in order:
             far_copy(1, g, k).wait_recv()
             other = yrecv2[(lon + k) % n_lon, offset:offset + size].astype(f32)
@@ -344,13 +361,27 @@
                 zsend2[k, offset:offset + size] = padded(value, size)
                 along_copy(1, g, k).start()
             else:
-                out_ref[0, first:first + count] = (value + b2_ref[...]).reshape(count, cols, width)
-    for g, (first, count, offset, size) in enumerate(blocks):
-        second = out_ref[0, first:first + count].reshape(count * cols, width)
+                out_ref[0, pl.ds(first_row(1, g), count)] = (value + b2_ref[...]).reshape(count, cols, width)
+
+    gather_one(0)
+    assemble_two(0)
+    weights_here(1, 1)
+    multiply_two(1, 0)
+    gather_one(1)
+    weights_here(1, 0)
+    multiply_two(0, 0)
+    assemble_two(1)
+    multiply_two(1, 1)
+    scatter_two(0)
+    multiply_two(0, 1)
+    scatter_two(1)
+    for g, (count, offset, size) in enumerate(blocks):
+        here = pl.ds(first_row(1, g), count)
+        second = out_ref[0, here].reshape(count * cols, width)
         for k in away:
             along_copy(1, g, k).wait_recv()
             second = second + zrecv2[k, offset:offset + size].astype(f32)[:count * cols]
-        out_ref[0, first:first + count] = second.reshape(count, cols, width)
+        out_ref[0, here] = second.reshape(count, cols, width)
 
     for k in order:
         forward_copy(k).wait_send()
@@ -383,7 +414,8 @@
     _, rows, cols, width = features.shape
     cells, part, all_cols = rows * cols, width // n_lon, cols * n_lon
     half = round_up(-(-cells // 2), 16)
-    band_half, tall = row_groups(rows, all_cols, 2)[1], row_groups(rows, cols, 1)[1]
+    counts = row_counts(rows)
+    band_half, tall = row_groups(counts[0], all_cols, 2)[1], row_groups(counts[1], cols, 1)[1]
     short = round_up(cols, 16)
     bf16, f32 = jnp.bfloat16, jnp.float32
     dma = pltpu.SemaphoreType.DMA

time: 44.8 us -> 43.8 us (0.978)
  Pallas kernels: 43 us -> 42.1 us
    pallas_call x1, Pallas kernels: 43 us -> 42.1 us  [body(): pl.pallas_call(functools.partial(block_kernel, n_lat, n_lon), out_shape=j...]
where the time goes in v5:
time: 43.8 us; the launch traced here: 43.7 us
  Pallas kernels  42.1 us (96%)
  other arithmetic  1.58 us (4%)
    pallas_call x1, Pallas kernels, body(): pl.pallas_call(functools.partial(block_kernel, n_lat, n_lon), out_shape=j...  42.1 us
    convert_element_type x1, other arithmetic, body(): return ((features.astype(f32) + second) * skip_scale).astype(bf16)  1.58 us

profile of v5, /device:TPU:0, one launch (start us, length us, event | category | flops | bytes accessed | tf_op | source)
XLA Modules:
  0.0 43.7 jit_solution(13518774206128945878)
XLA Ops:
  0.0 0.0 copy-start
  0.0 42.1 %residual_block.1 = f32[1,7,24,256]{3,2,1,0:T(8,128)} custom-call(bf16[1,7,24,256]{3,2,1,0:T(8,128)(2,1)} %x_ref.1, bf16[3,3,1,64,1024]{4,3,2,1,0:T(8,128)(2,1)} %k1_ref.1, f32[1,256]{1,0:T(1,128)} %bitcast.2, bf16[3,3,1,64,1024]{4,3,2,1,0:T(8,128)(2,1)} %k2_ref.1, f32[1,256]{1,0:T(1,128)} %bitcast.3), custom_call_target="tpu_custom_call" | custom-call | tf_op jit(solution)/shard_map/residual_block/pallas_call | solution.py:424
  42.1 0.0 copy-done
  42.1 1.6 %multiply_convert_fusion = bf16[1,7,24,256]{3,2,1,0:T(8,128)(2,1)} fusion(f32[1,7,24,256]{3,2,1,0:T(8,128)} %residual_block.1, bf16[1,7,24,256]{3,2,1,0:T(8,128)(2,1)S(1)} %copy-done), kind=kLoop, calls=%fused_computation | loop fusion | flops 172032 | bytes 344064 | tf_op jit(solution)/shard_map/convert_element_type | solution.py:463
Async XLA Ops:
  0.0 42.1 %copy-start = (bf16[1,7,24,256]{3,2,1,0:T(8,128)(2,1)S(1)}, bf16[1,7,24,256]{3,2,1,0:T(8,128)(2,1)}, u32[]{:S(2)}) copy-start(bf16[1,7,24,256]{3,2,1,0:T(8,128)(2,1)} %x_ref.1) | copy-start | bytes 258052

commit v6 on v5

--- a/solution.py
+++ b/solution.py
@@ -49,9 +49,9 @@
 
 def block_kernel(
     n_lat, n_lon, x_ref, k1_ref, b1_ref, k2_ref, b2_ref, out_ref,
-    w, apack, arecv, hpack, hrecv, bpack, brecv, epack, erecv, field, taps,
+    x_vmem, b1_vmem, b2_vmem, w, apack, arecv, bpack, brecv, epack, erecv, field, taps,
     own, kept, ysend1, yrecv1, zsend1, zrecv1, acc, ysend2, yrecv2, zsend2, zrecv2,
-    wl_sem, ws_sem, wr_sem, as_sem, ar_sem, hs_sem, hr_sem, fs_sem, fr_sem,
+    in_sem, wl_sem, ws_sem, wr_sem, as_sem, ar_sem,
     bs_sem, br_sem, es_sem, er_sem, ys_sem, yr_sem, zs_sem, zr_sem,
 ):
     rows, cols, width = x_ref.shape[1:]
@@ -95,18 +95,23 @@
             ),
         )
 
+    barrier = pltpu.get_barrier_semaphore()
+    greeted = 0
+    peers = [(0, along, ch) for along in away] + [(0, 0, near), (0, 0, far)]
+    peers += [(up, 0, channel) for up in sorted({1, n_lat - 1}) for channel in (ch, near)]
+    for peer in peers:
+        pl.semaphore_signal(barrier, inc=1, device_id=device(*peer), device_id_type=MESH)
+        greeted += 1
+
+    inputs = [
+        pltpu.make_async_copy(src, dst, in_sem.at[i])
+        for i, (src, dst) in enumerate(((x_ref, x_vmem), (b1_ref, b1_vmem), (b2_ref, b2_vmem)))
+    ]
+    for copy in inputs:
+        copy.start()
     weights = {(conv, slot): weight_copies(conv, slot) for conv in (0, 1) for slot in (1, 0)}
     for local, _ in weights.values():
         local.start()
-
-    barrier = pltpu.get_barrier_semaphore()
-    greeted = 0
-    ups = sorted({0, 1, n_lat - 1})
-    peers = [(up, along, ch) for up in ups for along in range(n_lon) if up or along]
-    peers += [(up, 0, near) for up in ups] + [(0, 0, far)]
-    for peer in peers:
-        pl.semaphore_signal(barrier, inc=1, device_id=device(*peer), device_id_type=MESH)
-        greeted += 1
 
     sends = (lat < n_lat - 1, lat > 0)
     gets = (lat > 0, lat < n_lat - 1)
@@ -122,24 +127,13 @@
             as_sem.at[1, k], ar_sem.at[1, k], device(0, 0, near),
         )
 
-    def halo_copy(side, k):
-        return remote(
-            hpack.at[side, (lon + k) % n_lon], hrecv.at[side, 0, k],
-            hs_sem.at[side, k], hr_sem.at[side, k], device((1, -1)[side] % n_lat, k, ch),
-        )
-
-    def halo_forward(side):
-        return remote(
-            hrecv.at[side, 0], hrecv.at[side, 1], fs_sem.at[side], fr_sem.at[side], device(0, 0, near)
-        )
-
     def band_copy(g):
         place = pl.ds(*bands[g][1:])
         return remote(bpack.at[place], brecv.at[place], bs_sem.at[g], br_sem.at[g], device(0, 0, near))
 
-    def edge_copy(side, p):
+    def edge_copy(conv, side, p):
         return remote(
-            epack.at[side], erecv.at[side, p], es_sem.at[side, p], er_sem.at[side, p],
+            epack.at[conv, side], erecv.at[conv, side, p], es_sem.at[conv, side, p], er_sem.at[conv, side, p],
             device((1, -1)[side] % n_lat, 0, (ch, near)[p]),
         )
 
@@ -171,14 +165,33 @@
 
     inside = slice(EDGE, EDGE + all_cols)
 
-    def fold(side):
-        row, inner = ((0, 1), (rows + 1, rows))[side]
-        turn = all_cols // 2
-        field[row, EDGE:EDGE + turn] = field[inner, EDGE + turn:EDGE + all_cols]
-        field[row, EDGE + turn:EDGE + all_cols] = field[inner, EDGE:EDGE + turn]
-
-    def spread(first, count):
-        here = pl.ds(first, count)
+    def send_edge(conv, side, edge, due=True):
+        @pl.when(jnp.logical_and(sends[side], due))
+        def _():
+            epack[conv, side] = edge.astype(bf16)
+            for p in (1, 0):
+                edge_copy(conv, side, p).start()
+
+    def close(conv, g):
+        for side in (0, 1):
+            due = jnp.logical_not(flip) if side == g else flip
+            row, inner = ((0, 1), (rows + 1, rows))[side]
+
+            @pl.when(jnp.logical_and(gets[side], due))
+            def _():
+                for p in (0, 1):
+                    edge_copy(conv, side, p).wait_recv()
+                    field[row, inside, lanes(p)] = erecv[conv, side, p].astype(f32)
+
+            @pl.when(jnp.logical_and(jnp.logical_not(gets[side]), due))
+            def _():
+                turn = all_cols // 2
+                field[row, EDGE:EDGE + turn] = field[inner, EDGE + turn:EDGE + all_cols]
+                field[row, EDGE + turn:EDGE + all_cols] = field[inner, EDGE:EDGE + turn]
+
+        ahead = counts[conv][0] + 2
+        behind = rows + 2 - ahead
+        here = pl.ds(jnp.where(flip, (behind, 0)[g], (0, ahead)[g]), (ahead, behind)[g])
         field[here, EDGE - 1:EDGE] = field[here, EDGE + all_cols - 1:EDGE + all_cols]
         field[here, EDGE + all_cols:EDGE + all_cols + 1] = field[here, EDGE:EDGE + 1]
         for e in range(3):
@@ -189,11 +202,6 @@
     def exchange_one():
         for k in away:
             main_copy(k).start()
-        for side in (0, 1):
-            @pl.when(sends[side])
-            def _():
-                for k in order:
-                    halo_copy(side, k).start()
         forward_copy(0).start()
 
     def assemble_one():
@@ -208,27 +216,12 @@
             main_copy(k).wait_recv()
             forward_copy(k).start()
             field[1:rows + 1, place(k), lanes(0)] = cell_block(arecv[0, k])
+        weights[0, 0][1].start()
         for side in (0, 1):
-            @pl.when(gets[side])
-            def _():
-                for k in order:
-                    halo_copy(side, k).wait_recv()
-                halo_forward(side).start()
+            send_edge(0, side, field[(rows, 1)[side], inside, lanes(0)])
         for k in [0] + away:
             forward_copy(k).wait_recv()
             field[1:rows + 1, place(k), lanes(1)] = cell_block(arecv[1, k])
-        for side in (0, 1):
-            @pl.when(gets[side])
-            def _():
-                halo_forward(side).wait_recv()
-                for p in (0, 1):
-                    for k in order:
-                        field[(0, rows + 1)[side], place(k), lanes(p)] = hrecv[side, p, k].astype(f32)[:cols]
-
-            @pl.when(jnp.logical_not(gets[side]))
-            def _():
-                fold(side)
-        spread(0, rows + 2)
 
     def hand_on(g, act):
         count, offset, size = bands[g]
@@ -237,12 +230,7 @@
         band = unpack(act, count * all_cols)
         for side in (0, 1):
             turned = flip if side == g else jnp.logical_not(flip)
-
-            @pl.when(jnp.logical_and(sends[side], turned))
-            def _():
-                epack[side] = (band[-all_cols:], band[:all_cols])[side].astype(bf16)
-                for p in (1, 0):
-                    edge_copy(side, p).start()
+            send_edge(1, side, (band[-all_cols:], band[:all_cols])[side], turned)
         field[pl.ds(first_row(0, g) + 1, count), inside, lanes(0)] = band.reshape(count, all_cols, part)
 
     def assemble_two(g):
@@ -250,20 +238,7 @@
         band_copy(g).wait_recv()
         other = unpack(brecv[offset:offset + size].astype(f32), count * all_cols)
         field[pl.ds(first_row(0, g) + 1, count), inside, lanes(1)] = other.reshape(count, all_cols, part)
-        for side in (0, 1):
-            due = jnp.logical_not(flip) if side == g else flip
-
-            @pl.when(jnp.logical_and(gets[side], due))
-            def _():
-                for p in (0, 1):
-                    edge_copy(side, p).wait_recv()
-                    field[(0, rows + 1)[side], inside, lanes(p)] = erecv[side, p].astype(f32)
-
-            @pl.when(jnp.logical_and(jnp.logical_not(gets[side]), due))
-            def _():
-                fold(side)
-        count += 1
-        spread(jnp.where(flip, (rows + 2 - count, 0)[g], (0, rows + 2 - count)[g]), count)
+        close(1, g)
 
     def weights_here(conv, slot):
         local, other = weights[conv, slot]
@@ -282,22 +257,19 @@
             total = term if total is None else total + term
         return total
 
-    features = x_ref[0].astype(f32).reshape(cells, width)
-    act = silu(features)
-    fill = jnp.zeros((hpack.shape[2] - cols, part), f32)
+    inputs[0].wait()
+    act = silu(x_vmem[0].astype(f32).reshape(cells, width))
     for j in range(n_lon):
-        piece = act[:, lanes(j)]
-        apack[j] = pack(piece, half).astype(bf16)
-        hpack[0, j] = jnp.concatenate([piece[cells - cols:], fill], axis=0).astype(bf16)
-        hpack[1, j] = jnp.concatenate([piece[:cols], fill], axis=0).astype(bf16)
+        apack[j] = pack(act[:, lanes(j)], half).astype(bf16)
     pl.semaphore_wait(barrier, greeted)
-    for slot in (1, 0):
-        weights[0, slot][1].start()
+    weights[0, 1][1].start()
     exchange_one()
     assemble_one()
 
-    weights_here(0, 1)
     for g, (_, offset, size) in enumerate(bands):
+        close(0, g)
+        if g == 0:
+            weights_here(0, 1)
         total = multiply(0, 1, g)
         for j in range(n_lon):
             ysend1[j, offset:offset + size] = pack(total[:, lanes(j)], size).astype(bf16)
@@ -320,9 +292,11 @@
                 along_copy(0, g, k).start()
             else:
                 kept[offset:offset + size] = value
-    bias = b1_ref[:, lanes(0)]
+    for copy in inputs[1:]:
+        copy.wait()
+    bias = b1_vmem[:, lanes(0)]
     for j in away:
-        bias = jnp.where(lon == j, b1_ref[:, lanes(j)], bias)
+        bias = jnp.where(lon == j, b1_vmem[:, lanes(j)], bias)
     bias = jnp.concatenate([bias, bias], axis=1)
 
     def chunk(slot, g, k):
@@ -361,7 +335,7 @@
                 zsend2[k, offset:offset + size] = padded(value, size)
                 along_copy(1, g, k).start()
             else:
-                out_ref[0, pl.ds(first_row(1, g), count)] = (value + b2_ref[...]).reshape(count, cols, width)
+                out_ref[0, pl.ds(first_row(1, g), count)] = (value + b2_vmem[...]).reshape(count, cols, width)
 
     gather_one(0)
     assemble_two(0)
@@ -389,17 +363,12 @@
             main_copy(k).wait_send()
     for g in (0, 1):
         band_copy(g).wait_send()
-    for side in (0, 1):
-        @pl.when(sends[side])
-        def _():
-            for k in order:
-                halo_copy(side, k).wait_send()
-            for p in (0, 1):
-                edge_copy(side, p).wait_send()
-
-        @pl.when(gets[side])
-        def _():
-            halo_forward(side).wait_send()
+    for conv in (0, 1):
+        for side in (0, 1):
+            @pl.when(sends[side])
+            def _():
+                for p in (0, 1):
+                    edge_copy(conv, side, p).wait_send()
     for conv in (0, 1):
         for slot in (0, 1):
             weights[conv, slot][1].wait_send()
@@ -416,7 +385,6 @@
     half = round_up(-(-cells // 2), 16)
     counts = row_counts(rows)
     band_half, tall = row_groups(counts[0], all_cols, 2)[1], row_groups(counts[1], cols, 1)[1]
-    short = round_up(cols, 16)
     bf16, f32 = jnp.bfloat16, jnp.float32
     dma = pltpu.SemaphoreType.DMA
     vmem = pl.BlockSpec(memory_space=pltpu.VMEM)
@@ -424,18 +392,19 @@
     second = pl.pallas_call(
         functools.partial(block_kernel, n_lat, n_lon),
         out_shape=jax.ShapeDtypeStruct(features.shape, f32),
-        in_specs=[vmem, anywhere, vmem, anywhere, vmem],
+        in_specs=[anywhere] * 5,
         out_specs=vmem,
         scratch_shapes=[
+            pltpu.VMEM(features.shape, bf16),
+            pltpu.VMEM((1, width), f32),
+            pltpu.VMEM((1, width), f32),
             pltpu.VMEM((2, 2, 3, 3, 2, part, width), bf16),
             pltpu.VMEM((n_lon, half, 2 * part), bf16),
             pltpu.VMEM((2, n_lon, half, 2 * part), bf16),
-            pltpu.VMEM((2, n_lon, short, part), bf16),
-            pltpu.VMEM((2, 2, n_lon, short, part), bf16),
             pltpu.VMEM((band_half, 2 * part), bf16),
             pltpu.VMEM((band_half, 2 * part), bf16),
-            pltpu.VMEM((2, all_cols, part), bf16),
             pltpu.VMEM((2, 2, all_cols, part), bf16),
+            pltpu.VMEM((2, 2, 2, all_cols, part), bf16),
             pltpu.VMEM((rows + 2, all_cols + 2 * EDGE, 2 * part), f32),
             pltpu.VMEM((rows + 2, all_cols, 6 * part), bf16),
             pltpu.VMEM((n_lon, band_half, 2 * part), f32),
@@ -449,10 +418,9 @@
             pltpu.VMEM((n_lon, tall, width), bf16),
             pltpu.VMEM((n_lon, tall, width), bf16),
             pltpu.VMEM((n_lon, tall, width), bf16),
-            dma((2, 2)), dma((2, 2)), dma((2, 2)),
+            dma((3,)), dma((2, 2)), dma((2, 2)), dma((2, 2)),
             dma((2, n_lon)), dma((2, n_lon)),
-            dma((2, n_lon)), dma((2, n_lon)), dma((2,)), dma((2,)),
-            dma((2,)), dma((2,)), dma((2, 2)), dma((2, 2)),
+            dma((2,)), dma((2,)), dma((2, 2, 2)), dma((2, 2, 2)),
             dma((2, 2, n_lon)), dma((2, 2, n_lon)), dma((2, 2, n_lon)), dma((2, 2, n_lon)),
         ],
         compiler_params=pltpu.CompilerParams(

time: 43.8 us -> 41.3 us (0.943)
  Pallas kernels: 42.1 us -> 39.6 us
    pallas_call x1, Pallas kernels: 42.1 us -> 39.6 us  [body(): pl.pallas_call(functools.partial(block_kernel, n_lat, n_lon), out_shape=j...]
where the time goes in v6:
time: 41.3 us; the launch traced here: 41.2 us
  Pallas kernels  39.6 us (96%)
  other arithmetic  1.58 us (4%)
    pallas_call x1, Pallas kernels, body(): pl.pallas_call(functools.partial(block_kernel, n_lat, n_lon), out_shape=j...  39.6 us
    convert_element_type x1, other arithmetic, body(): return ((features.astype(f32) + second) * skip_scale).astype(bf16)  1.58 us

profile of v6, /device:TPU:0, one launch (start us, length us, event | category | flops | bytes accessed | tf_op | source)
XLA Modules:
  0.0 41.2 jit_solution(4482938758852210487)
XLA Ops:
  0.0 0.0 copy-start
  0.0 39.6 %residual_block.1 = f32[1,7,24,256]{3,2,1,0:T(8,128)} custom-call(bf16[1,7,24,256]{3,2,1,0:T(8,128)(2,1)} %x_ref.1, bf16[3,3,1,64,1024]{4,3,2,1,0:T(8,128)(2,1)} %k1_ref.1, f32[1,256]{1,0:T(1,128)} %bitcast.2, bf16[3,3,1,64,1024]{4,3,2,1,0:T(8,128)(2,1)} %k2_ref.1, f32[1,256]{1,0:T(1,128)} %bitcast.3), custom_call_target="tpu_custom_call" | custom-call | tf_op jit(solution)/shard_map/residual_block/pallas_call | solution.py:392
  39.6 0.0 copy-done
  39.6 1.6 %multiply_convert_fusion = bf16[1,7,24,256]{3,2,1,0:T(8,128)(2,1)} fusion(f32[1,7,24,256]{3,2,1,0:T(8,128)} %residual_block.1, bf16[1,7,24,256]{3,2,1,0:T(8,128)(2,1)S(1)} %copy-done), kind=kLoop, calls=%fused_computation | loop fusion | flops 172032 | bytes 344064 | tf_op jit(solution)/shard_map/convert_element_type | solution.py:431
Async XLA Ops:
  0.0 39.6 %copy-start = (bf16[1,7,24,256]{3,2,1,0:T(8,128)(2,1)S(1)}, bf16[1,7,24,256]{3,2,1,0:T(8,128)(2,1)}, u32[]{:S(2)}) copy-start(bf16[1,7,24,256]{3,2,1,0:T(8,128)(2,1)} %x_ref.1) | copy-start | bytes 258052

commit v7 on v6

--- a/solution.py
+++ b/solution.py
@@ -325,9 +325,9 @@
             hidden = hidden + zrecv1[k, offset:offset + size].astype(f32)
         hand_on(g, silu(hidden + bias))
 
-    def scatter_two(g):
+    def scatter_two(g, steps):
         count, offset, size = blocks[g]
-        for k in order:
+        for k in steps:
             far_copy(1, g, k).wait_recv()
             other = yrecv2[(lon + k) % n_lon, offset:offset + size].astype(f32)
             value = chunk(0, g, k) + other[:count * cols]
@@ -341,14 +341,15 @@
     assemble_two(0)
     weights_here(1, 1)
     multiply_two(1, 0)
-    gather_one(1)
     weights_here(1, 0)
     multiply_two(0, 0)
+    gather_one(1)
+    scatter_two(0, away)
     assemble_two(1)
     multiply_two(1, 1)
-    scatter_two(0)
+    scatter_two(0, [0])
     multiply_two(0, 1)
-    scatter_two(1)
+    scatter_two(1, order)
     for g, (count, offset, size) in enumerate(blocks):
         here = pl.ds(first_row(1, g), count)
         second = out_ref[0, here].reshape(count * cols, width)
@@ -389,40 +390,41 @@
     dma = pltpu.SemaphoreType.DMA
     vmem = pl.BlockSpec(memory_space=pltpu.VMEM)
     anywhere = pl.BlockSpec(memory_space=pl.ANY)
+    scratch = [
+        pltpu.VMEM(features.shape, bf16),
+        pltpu.VMEM((1, width), f32),
+        pltpu.VMEM((1, width), f32),
+        pltpu.VMEM((2, 2, 3, 3, 2, part, width), bf16),
+        pltpu.VMEM((n_lon, half, 2 * part), bf16),
+        pltpu.VMEM((2, n_lon, half, 2 * part), bf16),
+        pltpu.VMEM((band_half, 2 * part), bf16),
+        pltpu.VMEM((band_half, 2 * part), bf16),
+        pltpu.VMEM((2, 2, all_cols, part), bf16),
+        pltpu.VMEM((2, 2, 2, all_cols, part), bf16),
+        pltpu.VMEM((rows + 2, all_cols + 2 * EDGE, 2 * part), f32),
+        pltpu.VMEM((rows + 2, all_cols, 6 * part), bf16),
+        pltpu.VMEM((n_lon, band_half, 2 * part), f32),
+        pltpu.VMEM((band_half, 2 * part), f32),
+        pltpu.VMEM((n_lon, band_half, 2 * part), bf16),
+        pltpu.VMEM((n_lon, band_half, 2 * part), bf16),
+        pltpu.VMEM((n_lon, band_half, 2 * part), bf16),
+        pltpu.VMEM((n_lon, band_half, 2 * part), bf16),
+        pltpu.VMEM((2, rows, all_cols, width), f32),
+        pltpu.VMEM((n_lon, tall, width), bf16),
+        pltpu.VMEM((n_lon, tall, width), bf16),
+        pltpu.VMEM((n_lon, tall, width), bf16),
+        pltpu.VMEM((n_lon, tall, width), bf16),
+        dma((3,)), dma((2, 2)), dma((2, 2)), dma((2, 2)),
+        dma((2, n_lon)), dma((2, n_lon)),
+        dma((2,)), dma((2,)), dma((2, 2, 2)), dma((2, 2, 2)),
+        dma((2, 2, n_lon)), dma((2, 2, n_lon)), dma((2, 2, n_lon)), dma((2, 2, n_lon)),
+    ]
     second = pl.pallas_call(
         functools.partial(block_kernel, n_lat, n_lon),
         out_shape=jax.ShapeDtypeStruct(features.shape, f32),
         in_specs=[anywhere] * 5,
         out_specs=vmem,
-        scratch_shapes=[
-            pltpu.VMEM(features.shape, bf16),
-            pltpu.VMEM((1, width), f32),
-            pltpu.VMEM((1, width), f32),
-            pltpu.VMEM((2, 2, 3, 3, 2, part, width), bf16),
-            pltpu.VMEM((n_lon, half, 2 * part), bf16),
-            pltpu.VMEM((2, n_lon, half, 2 * part), bf16),
-            pltpu.VMEM((band_half, 2 * part), bf16),
-            pltpu.VMEM((band_half, 2 * part), bf16),
-            pltpu.VMEM((2, 2, all_cols, part), bf16),
-            pltpu.VMEM((2, 2, 2, all_cols, part), bf16),
-            pltpu.VMEM((rows + 2, all_cols + 2 * EDGE, 2 * part), f32),
-            pltpu.VMEM((rows + 2, all_cols, 6 * part), bf16),
-            pltpu.VMEM((n_lon, band_half, 2 * part), f32),
-            pltpu.VMEM((band_half, 2 * part), f32),
-            pltpu.VMEM((n_lon, band_half, 2 * part), bf16),
-            pltpu.VMEM((n_lon, band_half, 2 * part), bf16),
-            pltpu.VMEM((n_lon, band_half, 2 * part), bf16),
-            pltpu.VMEM((n_lon, band_half, 2 * part), bf16),
-            pltpu.VMEM((2, rows, all_cols, width), f32),
-            pltpu.VMEM((n_lon, tall, width), bf16),
-            pltpu.VMEM((n_lon, tall, width), bf16),
-            pltpu.VMEM((n_lon, tall, width), bf16),
-            pltpu.VMEM((n_lon, tall, width), bf16),
-            dma((3,)), dma((2, 2)), dma((2, 2)), dma((2, 2)),
-            dma((2, n_lon)), dma((2, n_lon)),
-            dma((2,)), dma((2,)), dma((2, 2, 2)), dma((2, 2, 2)),
-            dma((2, 2, n_lon)), dma((2, 2, n_lon)), dma((2, 2, n_lon)), dma((2, 2, n_lon)),
-        ],
+        scratch_shapes=scratch,
         compiler_params=pltpu.CompilerParams(
             collective_id=0, has_side_effects=True, vmem_limit_bytes=56 * 2**20
         ),

time: 41.3 us -> 42.3 us (1.024)
  Pallas kernels: 39.6 us -> 40.5 us
    pallas_call x1, Pallas kernels: 39.6 us -> 40.5 us  [body(): pl.pallas_call(functools.partial(block_kernel, n_lat, n_lon), out_shape=j...]
where the time goes in v7:
time: 42.3 us; the launch traced here: 42.1 us
  Pallas kernels  40.5 us (96%)
  other arithmetic  1.58 us (4%)
    pallas_call x1, Pallas kernels, body(): pl.pallas_call(functools.partial(block_kernel, n_lat, n_lon), out_shape=j...  40.5 us
    convert_element_type x1, other arithmetic, body(): return ((features.astype(f32) + second) * skip_scale).astype(bf16)  1.58 us

profile of v7, /device:TPU:0, one launch (start us, length us, event | category | flops | bytes accessed | tf_op | source)
XLA Modules:
  0.0 42.1 jit_solution(8761392609476573221)
XLA Ops:
  0.0 0.0 copy-start
  0.0 40.5 %residual_block.1 = f32[1,7,24,256]{3,2,1,0:T(8,128)} custom-call(bf16[1,7,24,256]{3,2,1,0:T(8,128)(2,1)} %x_ref.1, bf16[3,3,1,64,1024]{4,3,2,1,0:T(8,128)(2,1)} %k1_ref.1, f32[1,256]{1,0:T(1,128)} %bitcast.2, bf16[3,3,1,64,1024]{4,3,2,1,0:T(8,128)(2,1)} %k2_ref.1, f32[1,256]{1,0:T(1,128)} %bitcast.3), custom_call_target="tpu_custom_call" | custom-call | tf_op jit(solution)/shard_map/residual_block/pallas_call | solution.py:422
  40.5 0.0 copy-done
  40.5 1.6 %multiply_convert_fusion = bf16[1,7,24,256]{3,2,1,0:T(8,128)(2,1)} fusion(f32[1,7,24,256]{3,2,1,0:T(8,128)} %residual_block.1, bf16[1,7,24,256]{3,2,1,0:T(8,128)(2,1)S(1)} %copy-done), kind=kLoop, calls=%fused_computation | loop fusion | flops 172032 | bytes 344064 | tf_op jit(solution)/shard_map/convert_element_type | solution.py:433
Async XLA Ops:
  0.0 40.5 %copy-start = (bf16[1,7,24,256]{3,2,1,0:T(8,128)(2,1)S(1)}, bf16[1,7,24,256]{3,2,1,0:T(8,128)(2,1)}, u32[]{:S(2)}) copy-start(bf16[1,7,24,256]{3,2,1,0:T(8,128)(2,1)} %x_ref.1) | copy-start | bytes 258052

commit v8 on v6

--- a/solution.py
+++ b/solution.py
@@ -68,7 +68,7 @@
     near = ch + 1 - 2 * (ch % 2)
     far = ch + 2 - 4 * ((ch // 2) % 2)
     near_far = near + 2 - 4 * ((near // 2) % 2)
-    away = list(range(1, n_lon))
+    away = sorted(range(1, n_lon), key=lambda k: abs(2 * k - n_lon))
     order = away + [0]
 
     def device(up, along, channel):
@@ -280,9 +280,6 @@
         total = multiply(0, 0, g)
         for j in range(n_lon):
             own[j, offset:offset + size] = pack(total[:, lanes(j)], size)
-    for slot in (1, 0):
-        weights[1, slot][1].start()
-    for g, (_, offset, size) in enumerate(bands):
         for k in order:
             far_copy(0, g, k).wait_recv()
             slot = (lon + k) % n_lon
@@ -292,6 +289,8 @@
                 along_copy(0, g, k).start()
             else:
                 kept[offset:offset + size] = value
+    for slot in (1, 0):
+        weights[1, slot][1].start()
     for copy in inputs[1:]:
         copy.wait()
     bias = b1_vmem[:, lanes(0)]

time: 41.3 us -> 40.9 us (level)
  no operation moved by 1% of the time
where the time goes in v8:
time: 40.9 us; the launch traced here: 40.8 us
  Pallas kernels  39.2 us (96%)
  other arithmetic  1.58 us (4%)
    pallas_call x1, Pallas kernels, body(): pl.pallas_call(functools.partial(block_kernel, n_lat, n_lon), out_shape=j...  39.2 us
    convert_element_type x1, other arithmetic, body(): return ((features.astype(f32) + second) * skip_scale).astype(bf16)  1.58 us

profile of v8, /device:TPU:0, one launch (start us, length us, event | category | flops | bytes accessed | tf_op | source)
XLA Modules:
  0.0 40.8 jit_solution(2949205824307305503)
XLA Ops:
  0.0 0.0 copy-start
  0.0 39.2 %residual_block.1 = f32[1,7,24,256]{3,2,1,0:T(8,128)} custom-call(bf16[1,7,24,256]{3,2,1,0:T(8,128)(2,1)} %x_ref.1, bf16[3,3,1,64,1024]{4,3,2,1,0:T(8,128)(2,1)} %k1_ref.1, f32[1,256]{1,0:T(1,128)} %bitcast.2, bf16[3,3,1,64,1024]{4,3,2,1,0:T(8,128)(2,1)} %k2_ref.1, f32[1,256]{1,0:T(1,128)} %bitcast.3), custom_call_target="tpu_custom_call" | custom-call | tf_op jit(solution)/shard_map/residual_block/pallas_call | solution.py:391
  39.2 0.0 copy-done
  39.2 1.6 %multiply_convert_fusion = bf16[1,7,24,256]{3,2,1,0:T(8,128)(2,1)} fusion(f32[1,7,24,256]{3,2,1,0:T(8,128)} %residual_block.1, bf16[1,7,24,256]{3,2,1,0:T(8,128)(2,1)S(1)} %copy-done), kind=kLoop, calls=%fused_computation | loop fusion | flops 172032 | bytes 344064 | tf_op jit(solution)/shard_map/convert_element_type | solution.py:430
Async XLA Ops:
  0.0 39.2 %copy-start = (bf16[1,7,24,256]{3,2,1,0:T(8,128)(2,1)S(1)}, bf16[1,7,24,256]{3,2,1,0:T(8,128)(2,1)}, u32[]{:S(2)}) copy-start(bf16[1,7,24,256]{3,2,1,0:T(8,128)(2,1)} %x_ref.1) | copy-start | bytes 258052
